TPU v7x, 256 devices: a whole 4x4x8 slice. The times are simulated.
256 devices in a mesh: seq: 32 (over z, x_hi, core), mp: 8 (over y, x_lo).
Axes of the slice: x: 4 (x_hi: 2, x_lo: 2; x = x_hi * 2 + x_lo), y: 4, z: 8, core: 2. Of those that a mesh axis runs over, the one named last changes fastest.
Arguments:
- anchor: bfloat16 [8192, 4608], P('seq', 'mp'), may hold values from -6 to 6
- augment: bfloat16 [8192, 2304], P('seq', 'mp'), may hold values from -6 to 6
- proj_weight: bfloat16 [2304, 4608], P(None, 'mp'), may hold values from -0.125 to 0.125
- q_weight: bfloat16 [4608, 2048], P(None, 'mp'), may hold values from -0.09375 to 0.09375
- kv_weight: bfloat16 [4608, 8, 2, 128], P(None, 'mp'), may hold values from -0.09375 to 0.09375
- doc_ids: int32 [8192], P('seq'), may hold values from 0 to 1, never falling along the last dimension, each value on 1 to 6144 neighbouring positions
- d_out: bfloat16 [8192, 2048], P('seq', 'mp'), may hold values from -6 to 6
Outputs:
- attended: bfloat16 [8192, 2048], P('seq', 'mp')
- grad_query: float32 [4608, 2048], P('seq', 'mp')
- grad_kv: float32 [4608, 8, 2, 128], P('seq', 'mp')
- grad_kv_rows: bfloat16 [8192, 8, 2, 128], P('seq', 'mp')
Inputs may be any that keep to these rules, and one draw needn't show every extreme that they name: `doc_ids`: document numbers never fall along the sequence; every document has 1 to 6144 tokens.
All inputs are finite; a program needn't handle non-finite values.
Results may differ from a plain program's by a relative error of at most 0.025.
Values may be sent and summed in bfloat16 or wider, within the bound.
A program may use at most 128 MiB of HBM per device.

v0:
```python
import math

import jax
import jax.numpy as jnp
from jax import lax
from jax.sharding import PartitionSpec as P

HD = 128


softcap_limit = 50.0
score_scale = 144.0 ** (-0.5)


def key_scores(query_heads, key_block, query_pos, key_pos, query_docs, key_docs):
    raw = (
        jnp.einsum("tkgd,ukd->kgtu", query_heads, key_block, preferred_element_type=jnp.float32)
        * score_scale
    )
    capped = softcap_limit * jnp.tanh(raw / softcap_limit)
    allowed = (key_pos[None, :] <= query_pos[:, None]) & (key_docs[None, :] == query_docs[:, None])
    weights = jnp.where(allowed, jnp.exp(capped), 0.0)
    return (capped, weights)


def score_grads(capped, weights, denom_heads, delta_heads, grad_heads, value_block):
    prob = weights / denom_heads[..., None]
    grad_prob = jnp.einsum(
        "tkgd,ukd->kgtu", grad_heads, value_block, preferred_element_type=jnp.float32
    )
    grad_soft = prob * (grad_prob - delta_heads[..., None])
    grad_raw = (grad_soft * (1.0 - (capped / softcap_limit) ** 2) * score_scale).astype(
        jnp.bfloat16
    )
    return (prob, grad_raw)


def body(anchor, augment, proj_weight, q_weight, kv_weight, doc_ids, d_out):
    rows = anchor.shape[0]
    whole_anchor, whole_aug = (
        lax.all_gather(anchor, "mp", axis=1, tiled=True),
        lax.all_gather(augment, "mp", axis=1, tiled=True),
    )
    projected_part = jnp.dot(whole_aug, proj_weight, preferred_element_type=jnp.float32).astype(
        jnp.bfloat16
    )
    projected = lax.all_gather(projected_part, "mp", axis=1, tiled=True)
    query = jnp.dot(whole_anchor, q_weight, preferred_element_type=jnp.float32).astype(jnp.bfloat16)
    kv_heads = kv_weight.shape[1]
    kv_flat = kv_weight.reshape(kv_weight.shape[0], -1)
    kv_local = jnp.dot(projected, kv_flat, preferred_element_type=jnp.float32).astype(jnp.bfloat16)
    kv_local = kv_local.reshape(rows, kv_heads, 2, HD)
    all_kv, all_docs = (
        lax.all_gather(kv_local, "seq", axis=0, tiled=True),
        lax.all_gather(doc_ids, "seq", axis=0, tiled=True),
    )
    total = all_kv.shape[0]
    group = query.shape[1] // (kv_heads * HD)
    query_heads = query.reshape(rows, kv_heads, group, HD)
    grad_heads = d_out.reshape(rows, kv_heads, group, HD)
    first_row = lax.axis_index("seq") * rows
    query_pos = first_row + jnp.arange(rows, dtype=jnp.int32)
    block = math.gcd(total, 2048)
    blocks = total // block
    kv_blocks = all_kv.reshape(blocks, block, kv_heads, 2, HD)
    doc_blocks = all_docs.reshape(blocks, block)
    block_ids = jnp.arange(blocks, dtype=jnp.int32)

    def forward_step(carry, inputs):
        numer, denom = carry
        kv_block, doc_block, block_id = inputs
        key_pos = block_id * block + jnp.arange(block, dtype=jnp.int32)
        capped, weights = key_scores(
            query_heads, kv_block[:, :, 0], query_pos, key_pos, doc_ids, doc_block
        )
        numer = numer + jnp.einsum(
            "kgtu,ukd->tkgd",
            weights.astype(jnp.bfloat16),
            kv_block[:, :, 1],
            preferred_element_type=jnp.float32,
        )
        denom = denom + jnp.sum(weights, axis=-1)
        return ((numer, denom), None)

    start_numer = jnp.zeros((rows, kv_heads, group, HD), jnp.float32)
    start_denom = jnp.zeros((kv_heads, group, rows), jnp.float32)
    (numer, denom), _ = lax.scan(
        forward_step, (start_numer, start_denom), (kv_blocks, doc_blocks, block_ids)
    )
    attended_heads = (numer / jnp.transpose(denom, (2, 0, 1))[..., None]).astype(jnp.bfloat16)
    attended = attended_heads.reshape(rows, -1)
    delta = jnp.sum(grad_heads.astype(jnp.float32) * attended_heads.astype(jnp.float32), axis=-1)
    delta_heads = jnp.transpose(delta, (1, 2, 0))

    def backward_step():

        def step(grad_total, inputs):
            kv_block, doc_block, block_id = inputs
            key_pos = block_id * block + jnp.arange(block, dtype=jnp.int32)
            capped, weights = key_scores(
                query_heads, kv_block[:, :, 0], query_pos, key_pos, doc_ids, doc_block
            )
            prob, grad_raw = score_grads(
                capped, weights, denom, delta_heads, grad_heads, kv_block[:, :, 1]
            )
            grad_total = grad_total + jnp.einsum(
                "kgtu,ukd->tkgd", grad_raw, kv_block[:, :, 0], preferred_element_type=jnp.float32
            )
            grad_key = jnp.einsum(
                "kgtu,tkgd->ukd", grad_raw, query_heads, preferred_element_type=jnp.float32
            )
            grad_value = jnp.einsum(
                "kgtu,tkgd->ukd",
                prob.astype(jnp.bfloat16),
                grad_heads,
                preferred_element_type=jnp.float32,
            )
            return (grad_total, jnp.stack([grad_key, grad_value], axis=2))

        return step

    grad_query_sum, terms = lax.scan(
        backward_step(), start_numer, (kv_blocks, doc_blocks, block_ids)
    )
    kv_grad = lax.psum_scatter(
        terms.reshape(total, kv_heads, 2, HD).astype(jnp.bfloat16),
        "seq",
        scatter_dimension=0,
        tiled=True,
    )
    grad_query_rows = grad_query_sum.astype(jnp.bfloat16).reshape(rows, -1)
    kv_grad_rows = kv_grad.reshape(rows, -1)
    query_term = jnp.einsum(
        "td,th->dh", whole_anchor, grad_query_rows, preferred_element_type=jnp.float32
    )
    kv_term = jnp.einsum("td,th->dh", projected, kv_grad_rows, preferred_element_type=jnp.float32)
    kv_term = kv_term.reshape(-1, kv_heads, 2, HD)
    grad_query, grad_kv = (
        lax.psum_scatter(
            query_term.astype(jnp.bfloat16), "seq", scatter_dimension=0, tiled=True
        ).astype(jnp.float32),
        lax.psum_scatter(
            kv_term.astype(jnp.bfloat16), "seq", scatter_dimension=0, tiled=True
        ).astype(jnp.float32),
    )
    return (attended, grad_query, grad_kv, kv_grad)


def solution(mesh):
    placed = (
        P("seq", "mp"),
        P("seq", "mp"),
        P(None, "mp"),
        P(None, "mp"),
        P(None, "mp", None, None),
        P("seq"),
        P("seq", "mp"),
    )
    return jax.shard_map(
        body,
        mesh=mesh,
        in_specs=placed,
        out_specs=(
            P("seq", "mp"),
            P("seq", "mp"),
            P("seq", "mp", None, None),
            P("seq", "mp", None, None),
        ),
        check_vma=False,
    )
```

profile of v0, /device:TPU:8, one launch (start us, length us, event | category | flops | bytes accessed | tf_op | source)
XLA Modules:
  0.0 920.2 jit_solution(17146060998733152237)
XLA Ops:
  8.0 46.6 %all-gather.6.cloned.1.call-done = bf16[256,2304]{0,1:T(8,128)(2,1)} async-done(((bf16[256,288]{0,1:T(8,128)(2,1)}), bf16[256,2304]{0,1:T(8,128)(2,1)}) %all-gather.6.cloned.1.call-update) | async-done | bytes 1179664 | tf_op jit(solution)/shard_map/all_gather | solution.py:42
  54.6 2.8 convolution_convert_fusion.2
  58.3 58.1 %all-gather.8.cloned.1.call-done = bf16[256,4608]{0,1:T(8,128)(2,1)} async-done(((bf16[256,576]{0,1:T(8,128)(2,1)}), bf16[256,4608]{0,1:T(8,128)(2,1)}) %all-gather.8.cloned.1.call-update) | async-done | bytes 2359312 | tf_op jit(solution)/shard_map/all_gather | solution.py:47
  116.4 3.4 fusion.39
  120.8 41.9 %all-gather = s32[32,1,256]{2,1,0:T(1,128)S(1)} all-gather(s32[1,1,256]{2,1,0:T(1,128)S(1)} %bitcast.264), channel_id=1, replica_groups=mesh['seq'=32,'mp'=8] {'seq'}, dimensions={0}, use_global_device_ids=true | all-gather | bytes 33792 | tf_op jit(solution)/shard_map/all_gather | solution.py:55
  163.5 13.8 %all-gather.12.cloned.1.call-done = bf16[256,4608]{0,1:T(8,128)(2,1)} async-done(((bf16[256,576]{0,1:T(8,128)(2,1)}), bf16[256,4608]{0,1:T(8,128)(2,1)}) %all-gather.12.cloned.1.call-update) | async-done | bytes 2359312 | tf_op jit(solution)/shard_map/all_gather | solution.py:41
  177.3 3.4 convolution_convert_fusion.3
  180.8 87.4 %all-gather.10.cloned.1.call-done = bf16[8192,1,2,128]{3,0,2,1:T(8,128)(2,1)} async-done(((bf16[256,1,2,128]{3,0,2,1:T(8,128)(2,1)}), bf16[8192,1,2,128]{3,0,2,1:T(8,128)(2,1)}) %all-gather.10.cloned.1.call-update) | async-done | bytes 4194320 | tf_op jit(solution)/shard_map/all_gather | solution.py:54
  268.3 4.4 copy.44
  272.7 37.0 %while.30 = (s32[]{:T(128)}, f32[256,1,2,128]{0,3,2,1:T(8,128)S(1)}, f32[1,2,256]{2,1,0:T(2,128)S(1)}, bf16[4,2048,1,2,128]{4,1,3,2,0:T(8,128)(2,1)}, s32[4]{0:T...) while((s32[]{:T(128)}, ...), condition=%wide.region_2.3_spmd.clone, body=%wide.region_0.2_spmd.clone.sunk | while | flops 543820544 | bytes 13290700 | solution.py:87
  275.4 1.4 compare_and_fusion.4
  276.9 2.8 fusion.68
  279.6 2.3 fusion.69
  282.0 1.3 dynamic-slice_bitcast_fusion.4
  284.7 1.4 compare_and_fusion.4
  286.1 2.8 fusion.68
  288.9 2.3 fusion.69
  293.9 1.4 compare_and_fusion.4
  295.4 2.8 fusion.68
  298.2 2.3 fusion.69
  303.2 1.4 compare_and_fusion.4
  304.7 2.8 fusion.68
  307.4 2.3 fusion.69
  309.8 67.1 %while.31 = (s32[]{:T(128)}, f32[256,1,2,128]{0,3,2,1:T(8,128)}, bf16[4,2048,1,2,128]{4,1,3,2,0:T(8,128)(2,1)}, bf16[4,2048,1,2,128]{4,1,3,2,0:T(8,128)(2,1)}, s...) while((s32[]{:T(128)}, f32[256,1,2,128]{0,3,2,1:T(8,128)}, ...), condition=%wide.region_5.6_spmd.clone, body=%wide.region_4.5_spmd.clone.sunk | while | flops 1362757888 | bytes 58770772 | solution.py:122
  313.3 1.4 compare_and_fusion.5
  314.8 3.4 fusion.78
  318.1 3.0 fusion.79
  321.1 3.7 convolution_bitcast_fusion.5
  330.1 1.4 compare_and_fusion.5
  331.5 3.3 fusion.78
  334.9 3.0 fusion.79
  337.9 3.7 convolution_bitcast_fusion.5
  346.8 1.4 compare_and_fusion.5
  348.3 3.4 fusion.78
  351.7 3.0 fusion.79
  354.7 3.7 convolution_bitcast_fusion.5
  363.6 1.4 compare_and_fusion.5
  365.1 3.3 fusion.78
  368.4 3.0 fusion.79
  371.4 3.7 convolution_bitcast_fusion.5
  377.0 10.4 %copy.50 = bf16[4,2048,1,2,128]{4,3,1,0,2:T(2,128)(2,1)} copy(bf16[4,2048,1,2,128]{4,1,3,2,0:T(8,128)(2,1)} %get-tuple-element.272) | data formatting | bytes 8388608 | tf_op jit(solution)/shard_map/convert_element_type | solution.py:126
  388.4 3.9 fusion.33
  392.2 4.3 copy.61
  397.9 268.5 %all-reduce.3.cloned.1.call-done = bf16[8192,1,2,128]{3,2,1,0:T(2,128)(2,1)} async-done(((bf16[8192,1,2,128]{3,2,1,0:T(2,128)(2,1)}), bf16[8192,1,2,128]{3,2,1,0:T(2,128)(2,1)}) %all-reduce.3.cloned.1.call-update) | async-done | bytes 4194320
  667.5 3.9 fusion.34
  672.2 117.3 %reduce-scatter.7.cloned.1.call-done = bf16[144,256]{1,0:T(8,128)(2,1)} async-done(((bf16[4608,256]{1,0:T(8,128)(2,1)}), bf16[144,256]{1,0:T(8,128)(2,1)}) %reduce-scatter.7.cloned.1.call-update) | async-done | bytes 73744
  791.3 120.5 %reduce-scatter.5.cloned.1.call-done = bf16[144,1,2,128]{3,0,2,1:T(8,128)(2,1)} async-done(((bf16[4608,1,2,128]{3,0,2,1:T(8,128)(2,1)}), bf16[144,1,2,128]{3,0,2,1:T(8,128)(2,1)}) %reduce-scatter.5.cloned.1.call-update) | async-done | bytes 73744 | tf_op jit(solution)/shard_map/reduce_scatter | solution.py:142
  911.8 1.6 copy.54
  (150 shorter events, 33.7 us)
Async XLA Ops:
  7.2 47.4 %copy-start = (bf16[2304,576]{0,1:T(8,128)(2,1)S(1)}, bf16[2304,576]{0,1:T(8,128)(2,1)}, u32[]{:S(2)}) copy-start(bf16[2304,576]{0,1:T(8,128)(2,1)} %param.13) | copy-start | bytes 7962628
  7.2 47.4 %all-gather.6.cloned.1.call-start = ((), (), s32[]{:S(2)}) async-start(), calls=%async_computation.2 | async-start | bytes 1327104 | tf_op jit(solution)/shard_map/all_gather | solution.py:42
  7.9 108.4 %all-gather.8.cloned.1.call-start = ((), (), s32[]{:S(2)}) async-start(), calls=%async_computation.3 | async-start | bytes 2654208 | tf_op jit(solution)/shard_map/all_gather | solution.py:47
  57.5 119.8 %all-gather.12.cloned.1.call-start = ((), (), s32[]{:S(2)}) async-start(), calls=%async_computation.5 | async-start | bytes 2654208 | tf_op jit(solution)/shard_map/all_gather | solution.py:41
  58.2 210.1 %all-gather.10.cloned.1.call-start = ((), (), s32[]{:S(2)}) async-start(), calls=%async_computation.4 | async-start | bytes 4325376 | tf_op jit(solution)/shard_map/all_gather | solution.py:54
  116.4 4.3 copy-start.7
  116.4 4.4 copy-start.10
  120.6 545.8 %all-reduce.3.cloned.1.call-start = ((), (), s32[]{:S(2)}) async-start(), calls=%async_computation.8 | async-start | bytes 8388608
  274.0 5.6 copy-start.4
  283.3 5.6 copy-start.4
  292.5 5.6 copy-start.4
  301.8 5.6 copy-start.4
  311.1 3.6 copy-start.3
  311.1 3.6 copy-start.8
  311.9 6.3 copy-start.2
  318.1 3.0 copy-start.9
  321.1 3.7 copy-start.1
  327.9 3.6 copy-start.3
  327.9 3.6 copy-start.8
  328.6 6.3 copy-start.2
  334.9 3.0 copy-start.9
  337.9 3.7 copy-start.1
  344.7 3.6 copy-start.3
  344.7 3.6 copy-start.8
  345.4 6.3 copy-start.2
  351.7 3.0 copy-start.9
  354.7 3.7 copy-start.1
  361.4 3.6 copy-start.3
  361.4 3.6 copy-start.8
  362.2 6.3 copy-start.2
  368.4 3.0 copy-start.9
  371.4 3.7 copy-start.1
  387.4 0.9 copy-start.5
  387.4 402.1 %reduce-scatter.7.cloned.1.call-start = ((), (), s32[]{:S(2)}) async-start(), calls=%async_computation.7 | async-start | bytes 2433024
  392.2 4.4 copy-start.11
  396.6 515.2 %reduce-scatter.5.cloned.1.call-start = ((), (), s32[]{:S(2)}) async-start(), calls=%async_computation.6 | async-start | bytes 2433024 | tf_op jit(solution)/shard_map/reduce_scatter | solution.py:142
  667.4 4.1 copy-start.6
Sparse Core Ops, SparseCore 0:
  9.8 44.7 all-gather.5
  57.6 58.7 all-gather.7
  118.2 59.1 all-gather.11
  180.6 87.6 all-gather.9
  387.5 278.8 all-reduce.2
  670.4 119.0 reduce-scatter.6
  794.3 117.4 reduce-scatter.4
where the time goes:
time: 922 us; the launch traced here: 920 us
  waiting for transfers between devices  714 us (77%)
  matrix products  83.4 us (9%)
  local copies, waits for them, and re-layouts  43.8 us (5%)
  blocking collectives  41.9 us (5%)
  other arithmetic  16.2 us (2%)
  between operations  15 us (2%)
    unnamed x9, waiting for transfers between devices  387 us
    reduce_scatter x1, waiting for transfers between devices, body(): lax.psum_scatter(kv_term.astype(jnp.bfloat16), 'seq', scatter_dimension=0...  121 us
    all_gather x1, waiting for transfers between devices, body(): lax.all_gather(kv_local, 'seq', axis=0, tiled=True)  87.4 us
    all_gather x1, waiting for transfers between devices, body(): projected = lax.all_gather(projected_part, 'mp', axis=1, tiled=True)  58.1 us
    all_gather x1, waiting for transfers between devices, body(): lax.all_gather(augment, 'mp', axis=1, tiled=True)  46.6 us
    all_gather x1, blocking collectives, body(): lax.all_gather(doc_ids, 'seq', axis=0, tiled=True)  41.9 us
  transfers between devices with their start and end apart: 7, of which 7 were waited for; matrix products, arithmetic and copies ran while one was open for 3% of the time, Pallas kernels for 0%

commit v1 on v0

v1 whole, which is shorter than its diff:
```python
import functools

import jax
import jax.numpy as jnp
from jax import lax
from jax.experimental import pallas as pl
from jax.experimental.pallas import tpu as pltpu
from jax.sharding import PartitionSpec as P

BF = jnp.bfloat16
F32 = jnp.float32
TOK = 256
HD = 128
MESH = pl.DeviceIdType.MESH
LOG2E = 1.4426950408889634
TN = (((0,), (0,)), ((), ()))


def remote(src, dst, send, recv, where):
    return pltpu.make_async_remote_copy(
        src_ref=src, dst_ref=dst, send_sem=send, recv_sem=recv, device_id=where, device_id_type=MESH
    )


def dot(a, b):
    return jnp.dot(a, b, preferred_element_type=F32)


def dot_tn(a, b):
    return lax.dot_general(a, b, TN, preferred_element_type=F32)


def rows_of(ref, start, size):
    return ref.at[pl.ds(pl.multiple_of(start, 16), size)]


def greet(partners):
    barrier = pltpu.get_barrier_semaphore()
    for where in partners:
        pl.semaphore_signal(barrier, inc=1, device_id=where, device_id_type=MESH)
    pl.semaphore_wait(barrier, len(partners))


class FeatureGather:
    def __init__(self, own, buf, rows, send, recv, m):
        self.own, self.buf, self.rows, self.send, self.recv = own, buf, rows, send, recv
        self.m = m
        self.p = m + 1 - 2 * lax.rem(m, 2)
        self.up, self.dn = lax.rem(m + 2, 8), lax.rem(m + 6, 8)

    def part(self, block, half=None):
        if half is None:
            return rows_of(self.buf, block * self.rows, self.rows)
        n = self.rows // 2
        return rows_of(self.buf, block * self.rows + half * n, n)

    def copy(self, i, src, dst, to):
        return remote(src, dst, self.send.at[i], self.recv.at[i], {"mp": to})

    def sent(self, i):
        m, p = self.m, self.p
        a, b = lax.rem(m + 6, 8), lax.rem(m + 2, 8)
        pa, pb = lax.rem(p + 6, 8), lax.rem(p + 2, 8)
        table = [
            (m, None, p), (m, None, self.up), (m, None, self.dn),
            (p, None, self.up), (p, None, self.dn),
            (a, 0, self.up), (b, 1, self.dn),
            (pa, 0, self.up), (pb, 1, self.dn),
        ]
        block, half, to = table[i]
        dst = self.part(block, half)
        return self.copy(i, self.own if i < 3 else dst, dst, to)

    def arrived(self, i):
        m, p = self.m, self.p
        o, po = lax.rem(m + 4, 8), lax.rem(p + 4, 8)
        table = [
            (p, None), (self.dn, None), (self.up, None),
            (lax.rem(p + 6, 8), None), (lax.rem(p + 2, 8), None),
            (o, 0), (o, 1), (po, 0), (po, 1),
        ]
        block, half = table[i]
        dst = self.part(block, half)
        return self.copy(i, dst, dst, p)

    def start(self):
        for i in range(3):
            self.sent(i).start()

    def relay(self, stage):
        if stage == 0:
            self.arrived(0).wait_recv()
            self.sent(3).start()
            self.sent(4).start()
        elif stage == 1:
            self.arrived(1).wait_recv()
            self.sent(5).start()
            self.arrived(2).wait_recv()
            self.sent(6).start()
        elif stage == 2:
            self.arrived(3).wait_recv()
            self.sent(7).start()
            self.arrived(4).wait_recv()
            self.sent(8).start()
        elif stage == 3:
            self.arrived(5).wait_recv()
            self.arrived(6).wait_recv()
        else:
            self.arrived(7).wait_recv()
            self.arrived(8).wait_recv()

    def blocks(self, stage):
        m, p = self.m, self.p
        return [
            [p], [self.dn, self.up], [lax.rem(p + 6, 8), lax.rem(p + 2, 8)],
            [lax.rem(m + 4, 8)], [lax.rem(p + 4, 8)],
        ][stage]

    def drain(self):
        for i in range(9):
            self.sent(i).wait_send()


def feature_kernel(
    aug_ref, anc_ref, pw_hbm, qw_hbm, kw_hbm, doc_ref,
    query_ref, kv_ref, first_ref, anchor_ref, projected_ref,
    augment, pw, qw, kw, acc, cnt_out, cnt_in,
    wsem, asend, arecv, nsend, nrecv, psend, precv, csend, crecv,
):
    s, m = lax.axis_index("seq"), lax.axis_index("mp")
    hyper = []
    for k in range(5):
        bit = lax.rem(s // (1 << k), 2)
        hyper.append(s + (1 << k) * (1 - 2 * bit))
    loads = [
        pltpu.make_async_copy(src, dst, wsem.at[i])
        for i, (src, dst) in enumerate([(pw_hbm, pw), (qw_hbm, qw), (kw_hbm, kw)])
    ]
    for load in loads:
        load.start()
    aug = FeatureGather(aug_ref, augment, 288, asend, arecv, m)
    anc = FeatureGather(anc_ref, anchor_ref, 576, nsend, nrecv, m)
    own_projected = rows_of(projected_ref, m * 576, 576)
    pro = FeatureGather(own_projected, projected_ref, 576, psend, precv, m)
    greet([{"mp": aug.p}, {"mp": aug.up}, {"mp": aug.dn}] + [{"seq": h} for h in hyper])
    aug.start()
    doc = doc_ref[...]
    zeros = jnp.sum((1 - doc).astype(F32), axis=1, keepdims=True)
    cnt_out[0] = jnp.broadcast_to(zeros, (8, 128)).astype(jnp.int32)
    step = lambda k: remote(cnt_out.at[k], cnt_in.at[k], csend.at[k], crecv.at[k], {"seq": hyper[k]})

    def count(k):
        step(k).wait_recv()
        cnt_out[k + 1] = cnt_out[k] + cnt_in[k]
        if k < 4:
            step(k + 1).start()

    step(0).start()
    anc.start()
    rows_of(augment, m * 288, 288)[...] = aug_ref[...]
    rows_of(anchor_ref, m * 576, 576)[...] = anc_ref[...]
    for stage in range(5):
        aug.relay(stage)
        count(stage)
    first_ref[...] = doc * cnt_out[5, 0:1, 0:1]
    loads[0].wait()
    own_projected[...] = dot(pw[...], augment[...]).astype(BF)
    pro.start()
    loads[1].wait()

    def add(buf, weight, block):
        acc[...] += dot_tn(rows_of(buf, block * 576, 576)[...], rows_of(weight, block * 576, 576)[...])

    acc[...] = jnp.zeros_like(acc)
    add(anchor_ref, qw, m)
    for stage in range(5):
        anc.relay(stage)
        if stage == 1:
            pro.relay(0)
        if stage == 3:
            pro.relay(1)
        for block in anc.blocks(stage):
            add(anchor_ref, qw, block)
    query_ref[...] = acc[...].astype(BF)
    loads[2].wait()
    acc[...] = jnp.zeros_like(acc)
    add(projected_ref, kw, m)
    for stage in range(5):
        if stage > 1:
            pro.relay(stage)
        for block in pro.blocks(stage):
            add(projected_ref, kw, block)
    kv_ref[...] = acc[...].astype(BF)
    aug.drain()
    anc.drain()
    pro.drain()
    for k in range(5):
        step(k).wait_send()


def feature_call(aug_t, anc_t, pw_t, q_weight, kv_flat, doc):
    dma = pltpu.SemaphoreType.DMA
    vmem = pl.BlockSpec(memory_space=pltpu.VMEM)
    hbm = pl.BlockSpec(memory_space=pl.ANY)
    return pl.pallas_call(
        feature_kernel,
        out_shape=[
            jax.ShapeDtypeStruct((TOK, 256), BF),
            jax.ShapeDtypeStruct((TOK, 256), BF),
            jax.ShapeDtypeStruct((1, TOK), jnp.int32),
            jax.ShapeDtypeStruct((4608, TOK), BF),
            jax.ShapeDtypeStruct((4608, TOK), BF),
        ],
        in_specs=[vmem, vmem, hbm, hbm, hbm, vmem],
        out_specs=[vmem] * 5,
        scratch_shapes=[
            pltpu.VMEM((2304, TOK), BF),
            pltpu.VMEM((576, 2304), BF),
            pltpu.VMEM((4608, 256), BF),
            pltpu.VMEM((4608, 256), BF),
            pltpu.VMEM((TOK, 256), F32),
            pltpu.VMEM((6, 8, 128), jnp.int32),
            pltpu.VMEM((5, 8, 128), jnp.int32),
            dma((3,)), dma((9,)), dma((9,)), dma((9,)), dma((9,)), dma((9,)), dma((9,)),
            dma((5,)), dma((5,)),
        ],
        compiler_params=pltpu.CompilerParams(
            collective_id=1, has_side_effects=True, vmem_limit_bytes=40 * 1024 * 1024
        ),
    )(aug_t, anc_t, pw_t, q_weight, kv_flat, doc)


def needed(t, z):
    return (t >= 0) & (z <= 7) & ((t >= 2) | (z <= 5))


def sequence_kernel(
    query_ref, kv_ref, dout_ref, first_ref, anchor_ref, projected_ref,
    att_ref, gq_ref, gkv_ref, rows_ref,
    kvs, q_n, q_t, do_n, do_t, num, den, first, place, delta, dq_t,
    mine, tosib, fromsib, ringout, ringin, xout, xin, grads,
    wsib_out, wsib_in, wd_out, wd_in, wu_out, wu_in, wx_out, wx_in, wacc,
    up_s, up_r, sb_s, sb_r, xp_s, xp_r, gs_s, gs_r, rg_s, rg_r, xg_s, xg_r,
    ws_s, ws_r, wd_s, wd_r, wu_s, wu_r, wx_s, wx_r,
):
    s = lax.axis_index("seq")
    z, xh, c = s // 4, lax.rem(s // 2, 2), lax.rem(s, 2)
    sib = {"seq": s + 1 - 2 * c}
    xp_id = s + 2 - 4 * xh
    xp = {"seq": xp_id}
    up, dn = {"seq": lax.rem(s + 4, 32)}, {"seq": lax.rem(s + 28, 32)}
    greet([sib, xp, up, dn])

    def block_copy(src, block, send, recv, where):
        return remote(src, kvs.at[block], send, recv, where)

    def lane(t, j):
        return 4 * t + 2 * j + c

    def to_up(g, j, src=None):
        b = lane(z - g, j)
        return block_copy(kvs.at[b] if src is None else src, b, up_s.at[g, j], up_r.at[g, j], up)

    def to_sib(g, j, src=None):
        b = lane(z - g, j)
        return block_copy(kvs.at[b] if src is None else src, b, sb_s.at[g, j], sb_r.at[g, j], sib)

    def from_sib(g, j):
        b = 4 * (z - g) + 2 * j + 1 - c
        return block_copy(kvs.at[b], b, sb_s.at[g, j], sb_r.at[g, j], sib)

    def from_dn(g, j):
        b = lane(z - g, j)
        return block_copy(kvs.at[b], b, up_s.at[g - 1, j], up_r.at[g - 1, j], dn)

    def up_needs(g):
        return needed(z - g, z + 1)

    to_xp = block_copy(kv_ref, s, xp_s, xp_r, xp)
    from_xp = block_copy(kvs.at[xp_id], xp_id, xp_s, xp_r, xp)
    to_xp.start()

    @pl.when(up_needs(0))
    def _():
        to_up(0, xh, kv_ref).start()

    to_sib(0, xh, kv_ref).start()
    kvs[s] = kv_ref[...]
    lanes = lax.broadcasted_iota(jnp.int32, (1, 2 * TOK), 1)
    place[...] = lax.rem(lanes, TOK) + s * TOK
    for h in range(2):
        cut = slice(h * TOK, (h + 1) * TOK)
        head = slice(h * HD, (h + 1) * HD)
        first[:, cut] = first_ref[...]
        q_n[cut, :] = query_ref[:, head]
        do_n[cut, :] = dout_ref[:, head]
        q_t[:, cut] = query_ref[:, head].T
        do_t[:, cut] = dout_ref[:, head].T
    num[...] = jnp.zeros_like(num)
    den[...] = jnp.zeros_like(den)
    dq_t[...] = jnp.zeros_like(dq_t)
    from_xp.wait_recv()

    @pl.when(up_needs(0))
    def _():
        to_up(0, 1 - xh).start()

    to_sib(0, 1 - xh).start()

    def scores(block):
        k, v = kvs[block, :, :HD], kvs[block, :, HD:]
        th = jnp.tanh(dot(k, q_t[...]) * (1.0 / 600.0))
        pos = block * TOK + lax.broadcasted_iota(jnp.int32, (TOK, 2 * TOK), 0)
        allowed = (pos >= first[...]) & (pos <= place[...])
        return k, v, th, jnp.where(allowed, jnp.exp2(th * (50.0 * LOG2E)), 0.0)

    def forward(g):
        def one(b, carry):
            block = 4 * (z - g) + b

            @pl.when(block <= s)
            def _():
                _, v, _, w = scores(block)
                den[...] += jnp.sum(w, axis=0, keepdims=True)
                num[...] += dot_tn(v, w.astype(BF))

            return carry

        lax.fori_loop(0, 4, one, 0)

    def forward_step(g, carry):
        @pl.when(needed(z - g, z))
        def _():
            @pl.when(g > 0)
            def _():
                for j in range(2):
                    from_dn(g, j).wait_recv()

                    @pl.when(up_needs(g))
                    def _():
                        to_up(g, j).start()

                    to_sib(g, j).start()

            for j in range(2):
                from_sib(g, j).wait_recv()
            forward(g)

        return carry

    lax.fori_loop(0, 6, forward_step, 0)

    attended = (num[...] * (1.0 / den[...])).astype(BF)
    delta[...] = jnp.sum(do_t[...].astype(F32) * attended.astype(F32), axis=0, keepdims=True)
    den[...] = 1.0 / den[...]
    for h in range(2):
        att_ref[:, h * HD:(h + 1) * HD] = attended[:, h * TOK:(h + 1) * TOK].T

    def ring_out(g, j):
        return remote(ringout.at[g - 1, j], ringin.at[g - 1, j], rg_s.at[g - 1, j], rg_r.at[g - 1, j], dn)

    def ring_in(g, j):
        return remote(ringout.at[g, j], ringin.at[g, j], rg_s.at[g, j], rg_r.at[g, j], up)

    def sib_grad(g, j):
        return remote(tosib.at[g, j], fromsib.at[g, j], gs_s.at[g, j], gs_r.at[g, j], sib)

    def backward(block, write):
        k, v, th, w = scores(block)
        prob = w * den[...]
        soft = prob * (dot(v, do_t[...]) - delta[...])
        raw = (soft * ((1.0 - th * th) * (1.0 / 12.0))).astype(BF)
        write(dot(raw, q_n[...]), dot(prob.astype(BF), do_n[...]))
        dq_t[...] += dot_tn(k, raw)

    def contributions(g):
        def for_sib(j, carry):
            block = 4 * (z - g) + 2 * j + 1 - c

            @pl.when(block <= s)
            def _():
                def write(gk, gv):
                    tosib[g, j, :, :HD] = gk.astype(BF)
                    tosib[g, j, :, HD:] = gv.astype(BF)

                backward(block, write)

            @pl.when(block > s)
            def _():
                tosib[g, j] = jnp.zeros((TOK, 256), BF)

            sib_grad(g, j).start()
            return carry

        def for_me(j, carry):
            block = lane(z - g, j)

            @pl.when(block <= s)
            def _():
                def write(gk, gv):
                    mine[j, :, :HD] = gk
                    mine[j, :, HD:] = gv

                backward(block, write)

            @pl.when(block > s)
            def _():
                mine[j] = jnp.zeros((TOK, 256), F32)

            return carry

        lax.fori_loop(0, 2, for_sib, 0)
        lax.fori_loop(0, 2, for_me, 0)

    def sum_up(g, j):
        sib_grad(g, j).wait_recv()
        mine[j] += fromsib[g, j].astype(F32)

        @pl.when(up_needs(g))
        def _():
            ring_in(g, j).wait_recv()
            mine[j] += ringin[g, j].astype(F32)

    def backward_step(i, carry):
        g = 5 - i

        @pl.when(needed(z - g, z))
        def _():
            contributions(g)
            for j in range(2):
                sum_up(g, j)
                ringout[g - 1, j] = mine[j].astype(BF)
                ring_out(g, j).start()

        return carry

    lax.fori_loop(0, 5, backward_step, 0)
    contributions(0)

    def weight(n, act):
        grad = grads.at[n]

        def partial(t, j, core):
            return dot(rows_of(act, t * 576 + j * 288 + core * 144, 144)[...], grad[...])

        def sib_copy(t):
            return remote(wsib_out.at[n, t], wsib_in.at[n, t], ws_s.at[n, t], ws_r.at[n, t], sib)

        def target(k, way):
            return lax.rem(z + 4 + k, 8) if way == 0 else lax.rem(z + 11 - k, 8)

        def send_all():
            def one(i, carry):
                t = lax.rem(z + 4 + 7 * lax.rem(i, 2) * (i // 2 + 1) + (1 - lax.rem(i, 2)) * (i // 2), 8)
                for j in range(2):
                    wsib_out[n, t, j] = partial(t, j, 1 - c).astype(BF)
                sib_copy(t).start()
                return carry

            lax.fori_loop(0, 8, one, 0)

        def hop(k, way):
            out, into = (wd_out, wd_in) if way == 0 else (wu_out, wu_in)
            ss, rr = (wd_s, wd_r) if way == 0 else (wu_s, wu_r)
            return remote(out.at[n, k], into.at[n, k], ss.at[n, k], rr.at[n, k], dn if way == 0 else up)

        def hop_step(k, way):
            out, into = (wd_out, wd_in) if way == 0 else (wu_out, wu_in)
            t = target(k, way)
            sib_copy(t).wait_recv()
            for j in range(2):
                wacc[j] = partial(t, j, c) + wsib_in[n, t, j].astype(F32)

            @pl.when(k > 0)
            def _():
                hop(k - 1, way).wait_recv()
                for j in range(2):
                    wacc[j] += into[n, k - 1, j].astype(F32)

            for j in range(2):
                out[n, k, j] = wacc[j].astype(BF)
            hop(k, way).start()

        def step(k):
            hop_step(k, 0)

            @pl.when(k < 3)
            def _():
                hop_step(k, 1)

        def x_copy():
            return remote(wx_out.at[n], wx_in.at[n], wx_s.at[n], wx_r.at[n], xp)

        def meet():
            sib_copy(z).wait_recv()
            hop(3, 0).wait_recv()
            hop(2, 1).wait_recv()
            for j in range(2):
                wacc[j] = (
                    partial(z, j, c) + wsib_in[n, z, j].astype(F32)
                    + wd_in[n, 3, j].astype(F32) + wu_in[n, 2, j].astype(F32)
                )
            wx_out[n] = wacc[1 - xh].astype(BF)
            x_copy().start()
            return wacc[xh]

        def drain():
            for t in range(8):
                sib_copy(t).wait_send()
            for k in range(4):
                hop(k, 0).wait_send()
            for k in range(3):
                hop(k, 1).wait_send()
            x_copy().wait_send()

        return send_all, step, meet, x_copy, drain

    wq = weight(0, anchor_ref)
    wkv = weight(1, projected_ref)
    for h in range(2):
        grads[0, :, h * HD:(h + 1) * HD] = dq_t[:, h * TOK:(h + 1) * TOK].T.astype(BF)
    wq[0]()
    wq[1](0)
    for j in range(2):
        sum_up(0, j)
    xout[...] = mine[1 - xh].astype(BF)
    x_rows = remote(xout, xin, xg_s, xg_r, xp)
    x_rows.start()
    wq[1](1)
    x_rows.wait_recv()
    grads[1] = (mine[xh] + xin[...].astype(F32)).astype(BF)
    rows_ref[...] = grads[1]
    wkv[0]()

    def both(k, carry):
        wkv[1](k)
        wq[1](k + 2)
        return carry

    lax.fori_loop(0, 2, both, 0)
    own_q = wq[2]()
    gq_ref[...] = own_q
    wkv[1](2)
    wkv[1](3)
    own_kv = wkv[2]()
    gkv_ref[...] = own_kv
    wq[3]().wait_recv()
    gq_ref[...] += wx_in[0].astype(F32)
    wkv[3]().wait_recv()
    gkv_ref[...] += wx_in[1].astype(F32)

    to_xp.wait_send()
    x_rows.wait_send()
    wq[4]()
    wkv[4]()

    def drained(g, carry):
        @pl.when(needed(z - g, z))
        def _():
            for j in range(2):
                to_sib(g, j).wait_send()
                sib_grad(g, j).wait_send()

                @pl.when(up_needs(g))
                def _():
                    to_up(g, j).wait_send()

                @pl.when(g > 0)
                def _():
                    ring_out(g, j).wait_send()

        return carry

    lax.fori_loop(0, 6, drained, 0)


def sequence_call(query, kv, d_out, first, anchor, projected):
    dma = pltpu.SemaphoreType.DMA
    vmem = pl.BlockSpec(memory_space=pltpu.VMEM)
    two = lambda n: [dma(n), dma(n)]
    return pl.pallas_call(
        sequence_kernel,
        out_shape=[
            jax.ShapeDtypeStruct((TOK, 256), BF),
            jax.ShapeDtypeStruct((144, 256), F32),
            jax.ShapeDtypeStruct((144, 256), F32),
            jax.ShapeDtypeStruct((TOK, 256), BF),
        ],
        in_specs=[vmem] * 6,
        out_specs=[vmem] * 4,
        scratch_shapes=[
            pltpu.VMEM((32, TOK, 256), BF),
            pltpu.VMEM((512, HD), BF), pltpu.VMEM((HD, 512), BF),
            pltpu.VMEM((512, HD), BF), pltpu.VMEM((HD, 512), BF),
            pltpu.VMEM((HD, 512), F32), pltpu.VMEM((1, 512), F32),
            pltpu.VMEM((1, 512), jnp.int32), pltpu.VMEM((1, 512), jnp.int32),
            pltpu.VMEM((1, 512), F32), pltpu.VMEM((HD, 512), F32),
            pltpu.VMEM((2, TOK, 256), F32),
            pltpu.VMEM((6, 2, TOK, 256), BF), pltpu.VMEM((6, 2, TOK, 256), BF),
            pltpu.VMEM((5, 2, TOK, 256), BF), pltpu.VMEM((5, 2, TOK, 256), BF),
            pltpu.VMEM((TOK, 256), BF), pltpu.VMEM((TOK, 256), BF),
            pltpu.VMEM((2, TOK, 256), BF),
            pltpu.VMEM((2, 8, 2, 144, 256), BF), pltpu.VMEM((2, 8, 2, 144, 256), BF),
            pltpu.VMEM((2, 4, 2, 144, 256), BF), pltpu.VMEM((2, 4, 2, 144, 256), BF),
            pltpu.VMEM((2, 3, 2, 144, 256), BF), pltpu.VMEM((2, 3, 2, 144, 256), BF),
            pltpu.VMEM((2, 144, 256), BF), pltpu.VMEM((2, 144, 256), BF),
            pltpu.VMEM((2, 144, 256), F32),
            *two((5, 2)), *two((6, 2)), *two(()), *two((6, 2)), *two((5, 2)), *two(()),
            *two((2, 8)), *two((2, 4)), *two((2, 3)), *two((2,)),
        ],
        compiler_params=pltpu.CompilerParams(
            collective_id=2, has_side_effects=True, vmem_limit_bytes=56 * 1024 * 1024
        ),
    )(query, kv, d_out, first, anchor, projected)


def body(anchor, augment, proj_weight, q_weight, kv_weight, doc_ids, d_out):
    query, kv, first, anchor_t, projected_t = feature_call(
        augment.T, anchor.T, proj_weight.T, q_weight,
        kv_weight.reshape(kv_weight.shape[0], -1), doc_ids.reshape(1, -1),
    )
    attended, grad_q, grad_kv, rows = sequence_call(query, kv, d_out, first, anchor_t, projected_t)
    return attended, grad_q, grad_kv.reshape(144, 1, 2, HD), rows.reshape(TOK, 1, 2, HD)


def solution(mesh):
    placed = (
        P("seq", "mp"), P("seq", "mp"), P(None, "mp"), P(None, "mp"),
        P(None, "mp", None, None), P("seq"), P("seq", "mp"),
    )
    return jax.shard_map(
        body,
        mesh=mesh,
        in_specs=placed,
        out_specs=(
            P("seq", "mp"), P("seq", "mp"),
            P("seq", "mp", None, None), P("seq", "mp", None, None),
        ),
        check_vma=False,
    )
```

time: 922 us -> 197 us (0.21)
  waiting for transfers between devices: 714 us -> 0 us
  Pallas kernels: 0 us -> 179 us
  matrix products: 83.4 us -> 0 us
  blocking collectives: 41.9 us -> 0 us
  local copies, waits for them, and re-layouts: 43.8 us -> 15.2 us
  other arithmetic: 16.2 us -> 0 us
  between operations: 15 us -> 0.7 us
    unnamed x9 -> x0, waiting for transfers between devices: 387 us -> none
    all_gather x4 -> x0, waiting for transfers between devices: 206 us -> none  [the longest x1 87.4 us: body(): lax.all_gather(kv_local, 'seq', axis=0, tiled=True)]
    pallas_call x0 -> x2, Pallas kernels: none -> 179 us  [the longest x1 115 us: sequence_call(): pl.pallas_call(sequence_kernel, out_shape=[jax.ShapeDtypeStruct((TOK, 256...]
    reduce_scatter x1 -> x0, waiting for transfers between devices: 121 us -> none  [body(): lax.psum_scatter(kv_term.astype(jnp.bfloat16), 'seq', scatter_dimension=0...]
    dot_general x33 -> x0, matrix products: 83.4 us -> none  [the longest x4 14.7 us: step(): jnp.einsum('kgtu,tkgd->ukd', prob.astype(jnp.bfloat16), grad_heads, prefe...]
    all_gather x1 -> x0, blocking collectives: 41.9 us -> none  [body(): lax.all_gather(doc_ids, 'seq', axis=0, tiled=True)]
    and x8 -> x0, other arithmetic: 11.6 us -> none  [key_scores(): (key_pos[None, :] <= query_pos[:, None]) & (key_docs[None, :] == query_do...]
    convert_element_type x1 -> x0, local copies, waits for them, and re-layouts: 10.4 us -> none  [body(): terms.reshape(total, kv_heads, 2, HD).astype(jnp.bfloat16)]
  transfers between devices with their start and end apart: 7 -> 0, of which waited for: 7 -> 0; matrix products, arithmetic and copies ran while one was open for 3% -> 0% of each run, Pallas kernels for 0% -> 0%
where the time goes in v1:
time: 197 us; the launch traced here: 195 us
  Pallas kernels  179 us (91%)
  local copies, waits for them, and re-layouts  15.2 us (8%)
    pallas_call x1, Pallas kernels, sequence_call(): pl.pallas_call(sequence_kernel, out_shape=[jax.ShapeDtypeStruct((TOK, 256...  115 us
    pallas_call x1, Pallas kernels, feature_call(): pl.pallas_call(feature_kernel, out_shape=[jax.ShapeDtypeStruct((TOK, 256)...  64.7 us
    unnamed x23, local copies, waits for them, and re-layouts  12 us

profile of v1, /device:TPU:8, one launch (start us, length us, event | category | flops | bytes accessed | tf_op | source)
XLA Modules:
  0.0 195.2 jit_solution(7051754710157127689)
XLA Ops:
  0.6 0.0 copy-start
  0.6 0.0 copy-start.4
  0.7 0.0 copy-start.5
  0.7 0.0 copy-start.8
  0.7 2.1 %copy.15 = bf16[576,8,2,128]{3,1,2,0:T(8,128)(2,1)S(1)} copy(bf16[576,8,2,128]{3,2,1,0:T(2,128)(2,1)} %bitcast.16) | data formatting | bytes 4718592
  2.8 0.3 copy-done
  3.1 0.0 copy-done.4
  3.1 0.0 copy-done.5
  3.1 0.0 copy-done.8
  3.1 0.0 copy-start.3
  3.1 1.7 copy-done.3
  4.8 64.7 %shard_map.102 = (bf16[256,256]{1,0:T(8,128)(2,1)S(1)}, bf16[256,256]{1,0:T(8,128)(2,1)S(1)}, s32[1,256]{1,0:T(1,128)S(1)}, bf16[4608,256]{1,0:T(8,128)(2,1)S(1)}, bf16[4608,256]{1,0:T(8,128)(2,1)S(1)}) custom-call(bf16[288,256]{1,0:T(8,128)(2,1)S(1)} %bitcast.14, bf16[576,256]{1,0:T(8,128)(2,1)S(1)} %bitcast.13, bf16[576,2304]{1,0:T(8,128)(2,1)S(1)} %bitcast.12, ...), custom_call_target="tpu_custom_call" | custom-call | tf_op jit(solution)/shard_map/pallas_call | solution.py:205
  69.5 0.0 copy-start.1
  69.5 1.4 copy-done.1
  70.9 0.0 copy-start.2
  70.9 1.4 copy-done.2
  72.3 0.0 copy-start.6
  72.3 0.7 copy-done.6
  73.0 0.0 copy-start.7
  73.0 0.7 copy-done.7
  73.6 0.0 copy-start.9
  73.6 0.6 copy-done.9
  74.2 114.7 %shard_map.103 = (bf16[256,256]{1,0:T(8,128)(2,1)}, f32[144,256]{1,0:T(8,128)}, f32[144,256]{1,0:T(8,128)}, bf16[256,256]{1,0:T(8,128)(2,1)}) custom-call(bf16[256,256]{1,0:T(8,128)(2,1)} %copy-done.6, bf16[256,256]{1,0:T(8,128)(2,1)} %copy-done.7, bf16[256,256]{1,0:T(8,128)(2,1)} %dout_ref.1, s32[1,256]{1,0:T(1,128)} %copy-done.9, ...), custom_call_target="tpu_custom_call" | custom-call | tf_op jit(solution)/shard_map/pallas_call | solution.py:581
  188.8 1.6 reshape.23
  190.4 1.6 reshape.22
  192.1 1.6 copy.18
  193.7 1.6 copy.19
Async XLA Ops:
  0.6 2.5 %copy-start = (bf16[2304,576]{0,1:T(8,128)(2,1)S(1)}, bf16[2304,576]{0,1:T(8,128)(2,1)}, u32[]{:S(2)}) copy-start(bf16[2304,576]{0,1:T(8,128)(2,1)} %param.9) | copy-start | bytes 7962628
  0.6 2.5 %copy-start.4 = (bf16[256,576]{0,1:T(8,128)(2,1)S(1)}, bf16[256,576]{0,1:T(8,128)(2,1)}, u32[]{:S(2)}) copy-start(bf16[256,576]{0,1:T(8,128)(2,1)} %param.7) | copy-start | bytes 884740
  0.7 2.5 %copy-start.5 = (bf16[256,288]{0,1:T(8,128)(2,1)S(1)}, bf16[256,288]{0,1:T(8,128)(2,1)}, u32[]{:S(2)}) copy-start(bf16[256,288]{0,1:T(8,128)(2,1)} %param.8) | copy-start | bytes 442372
  0.7 2.5 %copy-start.8 = (s32[256]{0:T(256)S(1)}, s32[256]{0:T(256)}, u32[]{:S(2)}) copy-start(s32[256]{0:T(256)} %param.12) | copy-start | bytes 3076
  3.1 1.7 copy-start.3
  69.5 1.4 copy-start.1
  70.9 1.4 copy-start.2
  72.3 0.7 copy-start.6
  73.0 0.7 copy-start.7
  73.6 0.6 copy-start.9

commit v2 on v1

--- a/solution.py
+++ b/solution.py
@@ -121,33 +121,50 @@
             self.sent(i).wait_send()
 
 
-def feature_kernel(
-    aug_ref, anc_ref, pw_hbm, qw_hbm, kw_hbm, doc_ref,
-    query_ref, kv_ref, first_ref, anchor_ref, projected_ref,
-    augment, pw, qw, kw, acc, cnt_out, cnt_in,
+def needed(t, z):
+    return (t >= 0) & (z <= 7) & ((t >= 2) | (z <= 5))
+
+
+def step_kernel(
+    aug_ref, anc_ref, pw_hbm, qw_hbm, kw_hbm, doc_ref, dout_ref,
+    att_ref, gq_ref, gkv_ref, rows_ref,
+    augment, anchor, projected, pw, qw, kw, kw_pairs, pairs, acc, kv_ref, cnt_out, cnt_in,
+    kvs, q_n, q_t, do_n, do_t, num, den, first, place, delta, dq_t,
+    mine, tosib, fromsib, ringout, ringin, xout, xin, grads,
+    wsib_out, wsib_in, wd_out, wd_in, wu_out, wu_in, wx_out, wx_in, wacc,
     wsem, asend, arecv, nsend, nrecv, psend, precv, csend, crecv,
+    up_s, up_r, sb_s, sb_r, xp_s, xp_r, gs_s, gs_r, rg_s, rg_r, xg_s, xg_r,
+    ws_s, ws_r, wd_s, wd_r, wu_s, wu_r, wx_s, wx_r,
 ):
     s, m = lax.axis_index("seq"), lax.axis_index("mp")
+    z, xh, c = s // 4, lax.rem(s // 2, 2), lax.rem(s, 2)
+    sib = {"seq": s + 1 - 2 * c}
+    xp_id = s + 2 - 4 * xh
+    xp = {"seq": xp_id}
+    up, dn = {"seq": lax.rem(s + 4, 32)}, {"seq": lax.rem(s + 28, 32)}
     hyper = []
     for k in range(5):
         bit = lax.rem(s // (1 << k), 2)
         hyper.append(s + (1 << k) * (1 - 2 * bit))
     loads = [
         pltpu.make_async_copy(src, dst, wsem.at[i])
-        for i, (src, dst) in enumerate([(pw_hbm, pw), (qw_hbm, qw), (kw_hbm, kw)])
+        for i, (src, dst) in enumerate([(pw_hbm, pw), (qw_hbm, qw), (kw_hbm, kw_pairs)])
     ]
     for load in loads:
         load.start()
     aug = FeatureGather(aug_ref, augment, 288, asend, arecv, m)
-    anc = FeatureGather(anc_ref, anchor_ref, 576, nsend, nrecv, m)
-    own_projected = rows_of(projected_ref, m * 576, 576)
-    pro = FeatureGather(own_projected, projected_ref, 576, psend, precv, m)
-    greet([{"mp": aug.p}, {"mp": aug.up}, {"mp": aug.dn}] + [{"seq": h} for h in hyper])
+    anc = FeatureGather(anc_ref, anchor, 576, nsend, nrecv, m)
+    own_projected = rows_of(projected, m * 576, 576)
+    pro = FeatureGather(own_projected, projected, 576, psend, precv, m)
+    greet([{"mp": aug.p}, {"mp": aug.up}, {"mp": aug.dn}, up, dn] + [{"seq": h} for h in hyper])
+
     aug.start()
     doc = doc_ref[...]
     zeros = jnp.sum((1 - doc).astype(F32), axis=1, keepdims=True)
     cnt_out[0] = jnp.broadcast_to(zeros, (8, 128)).astype(jnp.int32)
-    step = lambda k: remote(cnt_out.at[k], cnt_in.at[k], csend.at[k], crecv.at[k], {"seq": hyper[k]})
+
+    def step(k):
+        return remote(cnt_out.at[k], cnt_in.at[k], csend.at[k], crecv.at[k], {"seq": hyper[k]})
 
     def count(k):
         step(k).wait_recv()
@@ -156,146 +173,83 @@
             step(k + 1).start()
 
     step(0).start()
-    anc.start()
     rows_of(augment, m * 288, 288)[...] = aug_ref[...]
-    rows_of(anchor_ref, m * 576, 576)[...] = anc_ref[...]
+    rows_of(anchor, m * 576, 576)[...] = anc_ref[...]
+    loads[2].wait()
+
+    def unpair(i, carry):
+        pairs[...] = kw_pairs[pl.ds(pl.multiple_of(i * 1152, 1152), 1152), :].astype(F32)
+        for half in range(2):
+            out = pairs[pl.ds(half, 576, stride=2), :].astype(BF)
+            kw[pl.ds(pl.multiple_of(i * 576, 576), 576), half * HD:(half + 1) * HD] = out
+        return carry
+
     for stage in range(5):
         aug.relay(stage)
         count(stage)
-    first_ref[...] = doc * cnt_out[5, 0:1, 0:1]
-    loads[0].wait()
-    own_projected[...] = dot(pw[...], augment[...]).astype(BF)
-    pro.start()
-    loads[1].wait()
-
-    def add(buf, weight, block):
-        acc[...] += dot_tn(rows_of(buf, block * 576, 576)[...], rows_of(weight, block * 576, 576)[...])
-
-    acc[...] = jnp.zeros_like(acc)
-    add(anchor_ref, qw, m)
-    for stage in range(5):
-        anc.relay(stage)
-        if stage == 1:
-            pro.relay(0)
-        if stage == 3:
-            pro.relay(1)
-        for block in anc.blocks(stage):
-            add(anchor_ref, qw, block)
-    query_ref[...] = acc[...].astype(BF)
-    loads[2].wait()
-    acc[...] = jnp.zeros_like(acc)
-    add(projected_ref, kw, m)
-    for stage in range(5):
-        if stage > 1:
-            pro.relay(stage)
-        for block in pro.blocks(stage):
-            add(projected_ref, kw, block)
-    kv_ref[...] = acc[...].astype(BF)
-    aug.drain()
-    anc.drain()
-    pro.drain()
-    for k in range(5):
-        step(k).wait_send()
-
-
-def feature_call(aug_t, anc_t, pw_t, q_weight, kv_flat, doc):
-    dma = pltpu.SemaphoreType.DMA
-    vmem = pl.BlockSpec(memory_space=pltpu.VMEM)
-    hbm = pl.BlockSpec(memory_space=pl.ANY)
-    return pl.pallas_call(
-        feature_kernel,
-        out_shape=[
-            jax.ShapeDtypeStruct((TOK, 256), BF),
-            jax.ShapeDtypeStruct((TOK, 256), BF),
-            jax.ShapeDtypeStruct((1, TOK), jnp.int32),
-            jax.ShapeDtypeStruct((4608, TOK), BF),
-            jax.ShapeDtypeStruct((4608, TOK), BF),
-        ],
-        in_specs=[vmem, vmem, hbm, hbm, hbm, vmem],
-        out_specs=[vmem] * 5,
-        scratch_shapes=[
-            pltpu.VMEM((2304, TOK), BF),
-            pltpu.VMEM((576, 2304), BF),
-            pltpu.VMEM((4608, 256), BF),
-            pltpu.VMEM((4608, 256), BF),
-            pltpu.VMEM((TOK, 256), F32),
-            pltpu.VMEM((6, 8, 128), jnp.int32),
-            pltpu.VMEM((5, 8, 128), jnp.int32),
-            dma((3,)), dma((9,)), dma((9,)), dma((9,)), dma((9,)), dma((9,)), dma((9,)),
-            dma((5,)), dma((5,)),
-        ],
-        compiler_params=pltpu.CompilerParams(
-            collective_id=1, has_side_effects=True, vmem_limit_bytes=40 * 1024 * 1024
-        ),
-    )(aug_t, anc_t, pw_t, q_weight, kv_flat, doc)
-
-
-def needed(t, z):
-    return (t >= 0) & (z <= 7) & ((t >= 2) | (z <= 5))
-
-
-def sequence_kernel(
-    query_ref, kv_ref, dout_ref, first_ref, anchor_ref, projected_ref,
-    att_ref, gq_ref, gkv_ref, rows_ref,
-    kvs, q_n, q_t, do_n, do_t, num, den, first, place, delta, dq_t,
-    mine, tosib, fromsib, ringout, ringin, xout, xin, grads,
-    wsib_out, wsib_in, wd_out, wd_in, wu_out, wu_in, wx_out, wx_in, wacc,
-    up_s, up_r, sb_s, sb_r, xp_s, xp_r, gs_s, gs_r, rg_s, rg_r, xg_s, xg_r,
-    ws_s, ws_r, wd_s, wd_r, wu_s, wu_r, wx_s, wx_r,
-):
-    s = lax.axis_index("seq")
-    z, xh, c = s // 4, lax.rem(s // 2, 2), lax.rem(s, 2)
-    sib = {"seq": s + 1 - 2 * c}
-    xp_id = s + 2 - 4 * xh
-    xp = {"seq": xp_id}
-    up, dn = {"seq": lax.rem(s + 4, 32)}, {"seq": lax.rem(s + 28, 32)}
-    greet([sib, xp, up, dn])
-
-    def block_copy(src, block, send, recv, where):
-        return remote(src, kvs.at[block], send, recv, where)
-
-    def lane(t, j):
-        return 4 * t + 2 * j + c
-
-    def to_up(g, j, src=None):
-        b = lane(z - g, j)
-        return block_copy(kvs.at[b] if src is None else src, b, up_s.at[g, j], up_r.at[g, j], up)
-
-    def to_sib(g, j, src=None):
-        b = lane(z - g, j)
-        return block_copy(kvs.at[b] if src is None else src, b, sb_s.at[g, j], sb_r.at[g, j], sib)
-
-    def from_sib(g, j):
-        b = 4 * (z - g) + 2 * j + 1 - c
-        return block_copy(kvs.at[b], b, sb_s.at[g, j], sb_r.at[g, j], sib)
-
-    def from_dn(g, j):
-        b = lane(z - g, j)
-        return block_copy(kvs.at[b], b, up_s.at[g - 1, j], up_r.at[g - 1, j], dn)
-
-    def up_needs(g):
-        return needed(z - g, z + 1)
-
-    to_xp = block_copy(kv_ref, s, xp_s, xp_r, xp)
-    from_xp = block_copy(kvs.at[xp_id], xp_id, xp_s, xp_r, xp)
-    to_xp.start()
-
-    @pl.when(up_needs(0))
-    def _():
-        to_up(0, xh, kv_ref).start()
-
-    to_sib(0, xh, kv_ref).start()
-    kvs[s] = kv_ref[...]
+        lax.fori_loop(2 * stage, min(2 * stage + 2, 8), unpair, 0)
+    here = doc * cnt_out[5, 0:1, 0:1]
     lanes = lax.broadcasted_iota(jnp.int32, (1, 2 * TOK), 1)
     place[...] = lax.rem(lanes, TOK) + s * TOK
     for h in range(2):
         cut = slice(h * TOK, (h + 1) * TOK)
         head = slice(h * HD, (h + 1) * HD)
-        first[:, cut] = first_ref[...]
-        q_n[cut, :] = query_ref[:, head]
+        first[:, cut] = here
         do_n[cut, :] = dout_ref[:, head]
-        q_t[:, cut] = query_ref[:, head].T
         do_t[:, cut] = dout_ref[:, head].T
+    loads[0].wait()
+    loads[1].wait()
+    own_projected[...] = dot(pw[...], augment[...]).astype(BF)
+    pro.start()
+
+    def add(buf, weight, block):
+        acc[...] += dot_tn(rows_of(buf, block * 576, 576)[...], rows_of(weight, block * 576, 576)[...])
+
+    acc[...] = jnp.zeros_like(acc)
+    add(projected, kw, m)
+    for stage in range(5):
+        pro.relay(stage)
+        if stage == 2:
+            anc.start()
+        for block in pro.blocks(stage):
+            add(projected, kw, block)
+    kv_ref[...] = acc[...].astype(BF)
+
+    def block_copy(src, block, send, recv, where):
+        return remote(src, kvs.at[block], send, recv, where)
+
+    def lane(t, j):
+        return 4 * t + 2 * j + c
+
+    def to_up(g, j, src=None):
+        b = lane(z - g, j)
+        return block_copy(kvs.at[b] if src is None else src, b, up_s.at[g, j], up_r.at[g, j], up)
+
+    def to_sib(g, j, src=None):
+        b = lane(z - g, j)
+        return block_copy(kvs.at[b] if src is None else src, b, sb_s.at[g, j], sb_r.at[g, j], sib)
+
+    def from_sib(g, j):
+        b = 4 * (z - g) + 2 * j + 1 - c
+        return block_copy(kvs.at[b], b, sb_s.at[g, j], sb_r.at[g, j], sib)
+
+    def from_dn(g, j):
+        b = lane(z - g, j)
+        return block_copy(kvs.at[b], b, up_s.at[g - 1, j], up_r.at[g - 1, j], dn)
+
+    def up_needs(g):
+        return needed(z - g, z + 1)
+
+    to_xp = block_copy(kv_ref, s, xp_s, xp_r, xp)
+    from_xp = block_copy(kvs.at[xp_id], xp_id, xp_s, xp_r, xp)
+    to_xp.start()
+
+    @pl.when(up_needs(0))
+    def _():
+        to_up(0, xh, kv_ref).start()
+
+    to_sib(0, xh, kv_ref).start()
+    kvs[s] = kv_ref[...]
     num[...] = jnp.zeros_like(num)
     den[...] = jnp.zeros_like(den)
     dq_t[...] = jnp.zeros_like(dq_t)
@@ -328,19 +282,40 @@
 
         lax.fori_loop(0, 4, one, 0)
 
+    def pass_on(g):
+        for j in range(2):
+            from_dn(g, j).wait_recv()
+
+            @pl.when(up_needs(g))
+            def _():
+                to_up(g, j).start()
+
+            to_sib(g, j).start()
+
+    acc[...] = jnp.zeros_like(acc)
+    add(anchor, qw, m)
+    for stage in range(5):
+        anc.relay(stage)
+        for block in anc.blocks(stage):
+            add(anchor, qw, block)
+        if stage in (1, 2):
+            @pl.when(needed(z - stage, z))
+            def _():
+                pass_on(stage)
+
+    query = acc[...].astype(BF)
+    for h in range(2):
+        cut = slice(h * TOK, (h + 1) * TOK)
+        head = slice(h * HD, (h + 1) * HD)
+        q_n[cut, :] = query[:, head]
+        q_t[:, cut] = query[:, head].T
+
     def forward_step(g, carry):
         @pl.when(needed(z - g, z))
         def _():
-            @pl.when(g > 0)
-            def _():
-                for j in range(2):
-                    from_dn(g, j).wait_recv()
-
-                    @pl.when(up_needs(g))
-                    def _():
-                        to_up(g, j).start()
-
-                    to_sib(g, j).start()
+            @pl.when(g > 2)
+            def _():
+                pass_on(g)
 
             for j in range(2):
                 from_sib(g, j).wait_recv()
@@ -515,8 +490,8 @@
 
         return send_all, step, meet, x_copy, drain
 
-    wq = weight(0, anchor_ref)
-    wkv = weight(1, projected_ref)
+    wq = weight(0, anchor)
+    wkv = weight(1, projected)
     for h in range(2):
         grads[0, :, h * HD:(h + 1) * HD] = dq_t[:, h * TOK:(h + 1) * TOK].T.astype(BF)
     wq[0]()
@@ -529,7 +504,9 @@
     wq[1](1)
     x_rows.wait_recv()
     grads[1] = (mine[xh] + xin[...].astype(F32)).astype(BF)
-    rows_ref[...] = grads[1]
+    for half in range(2):
+        pairs[pl.ds(half, TOK, stride=2), :] = grads[1, :, half * HD:(half + 1) * HD].astype(F32)
+    rows_ref[...] = pairs[:2 * TOK, :].astype(BF)
     wkv[0]()
 
     def both(k, carry):
@@ -543,16 +520,23 @@
     wkv[1](2)
     wkv[1](3)
     own_kv = wkv[2]()
-    gkv_ref[...] = own_kv
+    wacc[0] = own_kv
     wq[3]().wait_recv()
     gq_ref[...] += wx_in[0].astype(F32)
     wkv[3]().wait_recv()
-    gkv_ref[...] += wx_in[1].astype(F32)
+    wacc[0] += wx_in[1].astype(F32)
+    for half in range(2):
+        gkv_ref[pl.ds(half, 144, stride=2), :] = wacc[0, :, half * HD:(half + 1) * HD]
 
     to_xp.wait_send()
     x_rows.wait_send()
     wq[4]()
     wkv[4]()
+    aug.drain()
+    anc.drain()
+    pro.drain()
+    for k in range(5):
+        step(k).wait_send()
 
     def drained(g, carry):
         @pl.when(needed(z - g, z))
@@ -574,21 +558,27 @@
     lax.fori_loop(0, 6, drained, 0)
 
 
-def sequence_call(query, kv, d_out, first, anchor, projected):
+def step_call(aug_t, anc_t, pw_t, q_weight, kv_pairs, doc, d_out):
     dma = pltpu.SemaphoreType.DMA
     vmem = pl.BlockSpec(memory_space=pltpu.VMEM)
+    hbm = pl.BlockSpec(memory_space=pl.ANY)
     two = lambda n: [dma(n), dma(n)]
     return pl.pallas_call(
-        sequence_kernel,
+        step_kernel,
         out_shape=[
             jax.ShapeDtypeStruct((TOK, 256), BF),
             jax.ShapeDtypeStruct((144, 256), F32),
-            jax.ShapeDtypeStruct((144, 256), F32),
-            jax.ShapeDtypeStruct((TOK, 256), BF),
+            jax.ShapeDtypeStruct((288, HD), F32),
+            jax.ShapeDtypeStruct((2 * TOK, HD), BF),
         ],
-        in_specs=[vmem] * 6,
+        in_specs=[vmem, vmem, hbm, hbm, hbm, vmem, vmem],
         out_specs=[vmem] * 4,
         scratch_shapes=[
+            pltpu.VMEM((2304, TOK), BF), pltpu.VMEM((4608, TOK), BF), pltpu.VMEM((4608, TOK), BF),
+            pltpu.VMEM((576, 2304), BF), pltpu.VMEM((4608, 256), BF), pltpu.VMEM((4608, 256), BF),
+            pltpu.VMEM((9216, HD), BF), pltpu.VMEM((1152, HD), F32),
+            pltpu.VMEM((TOK, 256), F32), pltpu.VMEM((TOK, 256), BF),
+            pltpu.VMEM((6, 8, 128), jnp.int32), pltpu.VMEM((5, 8, 128), jnp.int32),
             pltpu.VMEM((32, TOK, 256), BF),
             pltpu.VMEM((512, HD), BF), pltpu.VMEM((HD, 512), BF),
             pltpu.VMEM((512, HD), BF), pltpu.VMEM((HD, 512), BF),
@@ -605,21 +595,33 @@
             pltpu.VMEM((2, 3, 2, 144, 256), BF), pltpu.VMEM((2, 3, 2, 144, 256), BF),
             pltpu.VMEM((2, 144, 256), BF), pltpu.VMEM((2, 144, 256), BF),
             pltpu.VMEM((2, 144, 256), F32),
+            dma((3,)), *two((9,)), *two((9,)), *two((9,)), *two((5,)),
             *two((5, 2)), *two((6, 2)), *two(()), *two((6, 2)), *two((5, 2)), *two(()),
             *two((2, 8)), *two((2, 4)), *two((2, 3)), *two((2,)),
         ],
         compiler_params=pltpu.CompilerParams(
-            collective_id=2, has_side_effects=True, vmem_limit_bytes=56 * 1024 * 1024
+            collective_id=1, has_side_effects=True, vmem_limit_bytes=60 * 1024 * 1024
         ),
-    )(query, kv, d_out, first, anchor, projected)
+    )(aug_t, anc_t, pw_t, q_weight, kv_pairs, doc, d_out)
+
+
+def hand_over(*refs):
+    n = len(refs) // 2
+    for src, dst in zip(refs[:n], refs[n:]):
+        dst[...] = src[...]
 
 
 def body(anchor, augment, proj_weight, q_weight, kv_weight, doc_ids, d_out):
-    query, kv, first, anchor_t, projected_t = feature_call(
+    results = step_call(
         augment.T, anchor.T, proj_weight.T, q_weight,
-        kv_weight.reshape(kv_weight.shape[0], -1), doc_ids.reshape(1, -1),
+        kv_weight.reshape(-1, HD), doc_ids.reshape(1, -1), d_out,
     )
-    attended, grad_q, grad_kv, rows = sequence_call(query, kv, d_out, first, anchor_t, projected_t)
+    attended, grad_q, grad_kv, rows = pl.pallas_call(
+        hand_over,
+        out_shape=[jax.ShapeDtypeStruct(r.shape, r.dtype) for r in results],
+        in_specs=[pl.BlockSpec(memory_space=pltpu.VMEM)] * 4,
+        out_specs=[pl.BlockSpec(memory_space=pltpu.VMEM)] * 4,
+    )(*results)
     return attended, grad_q, grad_kv.reshape(144, 1, 2, HD), rows.reshape(TOK, 1, 2, HD)
 
 

time: 197 us -> 164 us (0.83)
  Pallas kernels: 179 us -> 162 us
  local copies, waits for them, and re-layouts: 15.2 us -> 0 us
    pallas_call x2, Pallas kernels: 179 us -> 162 us  [the longest x1 160 us: step_call(): pl.pallas_call(step_kernel, out_shape=[jax.ShapeDtypeStruct((TOK, 256), B...]
    unnamed x23 -> x0, local copies, waits for them, and re-layouts: 12 us -> none
    reshape x2 -> x0, local copies, waits for them, and re-layouts: 3.24 us -> none  [the longest x1 1.64 us: body(): grad_kv.reshape(144, 1, 2, HD)]
where the time goes in v2:
time: 164 us; the launch traced here: 163 us
  Pallas kernels  162 us (99%)
    pallas_call x1, Pallas kernels, step_call(): pl.pallas_call(step_kernel, out_shape=[jax.ShapeDtypeStruct((TOK, 256), B...  160 us

profile of v2, /device:TPU:8, one launch (start us, length us, event | category | flops | bytes accessed | tf_op | source)
XLA Modules:
  0.0 162.7 jit_solution(7802623558625446326)
XLA Ops:
  0.6 160.2 %shard_map.102 = (bf16[256,256]{1,0:T(8,128)(2,1)}, f32[144,256]{1,0:T(8,128)}, f32[288,128]{1,0:T(8,128)}, bf16[512,128]{1,0:T(8,128)(2,1)}) custom-call(bf16[288,256]{1,0:T(8,128)(2,1)} %bitcast.14, bf16[576,256]{1,0:T(8,128)(2,1)} %bitcast.13, bf16[576,2304]{1,0:T(8,128)(2,1)} %bitcast.11, bf16[4608,256]{1,0:T(8,128)(2,1)} %qw_hbm.1, ...), custom_call_target="tpu_custom_call" | custom-call | tf_op jit(solution)/shard_map/pallas_call | solution.py:566
  160.8 1.9 %shard_map.103 = (bf16[256,256]{1,0:T(8,128)(2,1)}, f32[144,256]{1,0:T(8,128)}, f32[288,128]{1,0:T(8,128)}, bf16[512,128]{1,0:T(8,128)(2,1)}) custom-call(bf16[256,256]{1,0:T(8,128)(2,1)} %get-tuple-element.12.refs_0_, f32[144,256]{1,0:T(8,128)} %get-tuple-element.13.refs_1_, f32[288,128]{1,0:T(8,128)} %get-tuple-element.14.refs_2_, ...), custom_call_target="tpu_custom_call" | custom-call | tf_op jit(solution)/shard_map/pallas_call | solution.py:619

commit v3 on v2

--- a/solution.py
+++ b/solution.py
@@ -10,6 +10,7 @@
 BF = jnp.bfloat16
 F32 = jnp.float32
 TOK = 256
+HALF = 128
 HD = 128
 MESH = pl.DeviceIdType.MESH
 LOG2E = 1.4426950408889634
@@ -42,17 +43,17 @@
 
 
 class FeatureGather:
-    def __init__(self, own, buf, rows, send, recv, m):
+    def __init__(self, own, buf, rows, send, recv, m, lanes=pl.ds(0, TOK)):
         self.own, self.buf, self.rows, self.send, self.recv = own, buf, rows, send, recv
+        self.lanes = lanes
         self.m = m
         self.p = m + 1 - 2 * lax.rem(m, 2)
         self.up, self.dn = lax.rem(m + 2, 8), lax.rem(m + 6, 8)
 
     def part(self, block, half=None):
-        if half is None:
-            return rows_of(self.buf, block * self.rows, self.rows)
-        n = self.rows // 2
-        return rows_of(self.buf, block * self.rows + half * n, n)
+        n = self.rows if half is None else self.rows // 2
+        start = block * self.rows + (half or 0) * n
+        return self.buf.at[pl.ds(pl.multiple_of(start, 16), n), self.lanes]
 
     def copy(self, i, src, dst, to):
         return remote(src, dst, self.send.at[i], self.recv.at[i], {"mp": to})
@@ -155,8 +156,16 @@
     aug = FeatureGather(aug_ref, augment, 288, asend, arecv, m)
     anc = FeatureGather(anc_ref, anchor, 576, nsend, nrecv, m)
     own_projected = rows_of(projected, m * 576, 576)
-    pro = FeatureGather(own_projected, projected, 576, psend, precv, m)
-    greet([{"mp": aug.p}, {"mp": aug.up}, {"mp": aug.dn}, up, dn] + [{"seq": h} for h in hyper])
+    halves = [pl.ds(h * HALF, HALF) for h in range(2)]
+    pros = [
+        FeatureGather(own_projected.at[:, half], projected, 576, psend.at[h], precv.at[h], m, half)
+        for h, half in enumerate(halves)
+    ]
+    far, near = {"seq": lax.rem(s + 20, 32)}, {"seq": lax.rem(s + 12, 32)}
+    greet(
+        [{"mp": aug.p}, {"mp": aug.up}, {"mp": aug.dn}, up, dn, far, near]
+        + [{"seq": h} for h in hyper]
+    )
 
     aug.start()
     doc = doc_ref[...]
@@ -199,67 +208,104 @@
         do_t[:, cut] = dout_ref[:, head].T
     loads[0].wait()
     loads[1].wait()
-    own_projected[...] = dot(pw[...], augment[...]).astype(BF)
-    pro.start()
-
-    def add(buf, weight, block):
-        acc[...] += dot_tn(rows_of(buf, block * 576, 576)[...], rows_of(weight, block * 576, 576)[...])
-
-    acc[...] = jnp.zeros_like(acc)
-    add(projected, kw, m)
-    for stage in range(5):
-        pro.relay(stage)
-        if stage == 2:
-            anc.start()
-        for block in pro.blocks(stage):
-            add(projected, kw, block)
-    kv_ref[...] = acc[...].astype(BF)
-
-    def block_copy(src, block, send, recv, where):
-        return remote(src, kvs.at[block], send, recv, where)
+    for h, half in enumerate(halves):
+        own_projected[:, half] = dot(pw[...], augment[:, half]).astype(BF)
+        if h == 0:
+            pros[0].start()
+
+    def add(block):
+        acc[...] += dot_tn(rows_of(anchor, block * 576, 576)[...], rows_of(qw, block * 576, 576)[...])
+
+    def add_kv(h, block):
+        piece = projected[pl.ds(pl.multiple_of(block * 576, 16), 576), halves[h]]
+        acc[halves[h]] += dot_tn(piece, rows_of(kw, block * 576, 576)[...])
+
+    def half_copy(src, block, h, send, recv, where):
+        dst = kvs.at[block, halves[h]]
+        return remote(dst if src is None else src.at[halves[h]], dst, send, recv, where)
 
     def lane(t, j):
         return 4 * t + 2 * j + c
 
-    def to_up(g, j, src=None):
-        b = lane(z - g, j)
-        return block_copy(kvs.at[b] if src is None else src, b, up_s.at[g, j], up_r.at[g, j], up)
-
-    def to_sib(g, j, src=None):
-        b = lane(z - g, j)
-        return block_copy(kvs.at[b] if src is None else src, b, sb_s.at[g, j], sb_r.at[g, j], sib)
-
-    def from_sib(g, j):
+    def to_up(g, j, h, src=None):
+        return half_copy(src, lane(z - g, j), h, up_s.at[g, j, h], up_r.at[g, j, h], up)
+
+    def to_far(j, h, src=None):
+        return half_copy(src, lane(z, j), h, up_s.at[4, j, h], up_r.at[4, j, h], far)
+
+    def to_sib(g, j, h, src=None):
+        return half_copy(src, lane(z - g, j), h, sb_s.at[g, j, h], sb_r.at[g, j, h], sib)
+
+    def from_sib(g, j, h):
         b = 4 * (z - g) + 2 * j + 1 - c
-        return block_copy(kvs.at[b], b, sb_s.at[g, j], sb_r.at[g, j], sib)
-
-    def from_dn(g, j):
-        b = lane(z - g, j)
-        return block_copy(kvs.at[b], b, up_s.at[g - 1, j], up_r.at[g - 1, j], dn)
+        return half_copy(None, b, h, sb_s.at[g, j, h], sb_r.at[g, j, h], sib)
+
+    def from_dn(g, j, h):
+        return half_copy(None, lane(z - g, j), h, up_s.at[g - 1, j, h], up_r.at[g - 1, j, h], dn)
 
     def up_needs(g):
-        return needed(z - g, z + 1)
-
-    to_xp = block_copy(kv_ref, s, xp_s, xp_r, xp)
-    from_xp = block_copy(kvs.at[xp_id], xp_id, xp_s, xp_r, xp)
-    to_xp.start()
-
-    @pl.when(up_needs(0))
-    def _():
-        to_up(0, xh, kv_ref).start()
-
-    to_sib(0, xh, kv_ref).start()
-    kvs[s] = kv_ref[...]
+        return (g < 4) & needed(z - g, z + 1)
+
+    far_needs = needed(z, z + 5)
+
+    def to_xp(h):
+        return half_copy(kv_ref, s, h, xp_s.at[h], xp_r.at[h], xp)
+
+    def from_xp(h):
+        return half_copy(None, xp_id, h, xp_s.at[h], xp_r.at[h], xp)
+
+    def spread(j, h, src=None):
+        @pl.when(up_needs(0))
+        def _():
+            to_up(0, j, h, src).start()
+
+        @pl.when(far_needs)
+        def _():
+            to_far(j, h, src).start()
+
+        to_sib(0, j, h, src).start()
+
+    def launch(h):
+        kv_ref[halves[h]] = acc[halves[h]].astype(BF)
+        to_xp(h).start()
+        spread(xh, h, kv_ref)
+        kvs[s, halves[h]] = kv_ref[halves[h]]
+
+    def second(h):
+        from_xp(h).wait_recv()
+        spread(1 - xh, h)
+
+    def pass_on(g, h):
+        @pl.when(needed(z - g, z))
+        def _():
+            for j in range(2):
+                from_dn(g, j, h).wait_recv()
+
+                @pl.when(up_needs(g))
+                def _():
+                    to_up(g, j, h).start()
+
+                to_sib(g, j, h).start()
+
+    acc[...] = jnp.zeros_like(acc)
+    for h in range(2):
+        add_kv(h, m)
+        for stage in range(5):
+            pros[h].relay(stage)
+            if stage == 2:
+                if h == 0:
+                    pros[1].start()
+                else:
+                    anc.start()
+                    second(0)
+            for block in pros[h].blocks(stage):
+                add_kv(h, block)
+        launch(h)
+    pass_on(1, 0)
     num[...] = jnp.zeros_like(num)
     den[...] = jnp.zeros_like(den)
     dq_t[...] = jnp.zeros_like(dq_t)
-    from_xp.wait_recv()
-
-    @pl.when(up_needs(0))
-    def _():
-        to_up(0, 1 - xh).start()
-
-    to_sib(0, 1 - xh).start()
+    second(1)
 
     def scores(block):
         k, v = kvs[block, :, :HD], kvs[block, :, HD:]
@@ -282,26 +328,14 @@
 
         lax.fori_loop(0, 4, one, 0)
 
-    def pass_on(g):
-        for j in range(2):
-            from_dn(g, j).wait_recv()
-
-            @pl.when(up_needs(g))
-            def _():
-                to_up(g, j).start()
-
-            to_sib(g, j).start()
-
     acc[...] = jnp.zeros_like(acc)
-    add(anchor, qw, m)
+    add(m)
     for stage in range(5):
         anc.relay(stage)
         for block in anc.blocks(stage):
-            add(anchor, qw, block)
-        if stage in (1, 2):
-            @pl.when(needed(z - stage, z))
-            def _():
-                pass_on(stage)
+            add(block)
+        if stage < 3:
+            pass_on((stage + 3) // 2, (stage + 1) % 2)
 
     query = acc[...].astype(BF)
     for h in range(2):
@@ -315,10 +349,12 @@
         def _():
             @pl.when(g > 2)
             def _():
-                pass_on(g)
-
-            for j in range(2):
-                from_sib(g, j).wait_recv()
+                for h in range(2):
+                    pass_on(g, h)
+
+            for h in range(2):
+                for j in range(2):
+                    from_sib(g, j, h).wait_recv()
             forward(g)
 
         return carry
@@ -331,8 +367,8 @@
     for h in range(2):
         att_ref[:, h * HD:(h + 1) * HD] = attended[:, h * TOK:(h + 1) * TOK].T
 
-    def ring_out(g, j):
-        return remote(ringout.at[g - 1, j], ringin.at[g - 1, j], rg_s.at[g - 1, j], rg_r.at[g - 1, j], dn)
+    def ring_out(g, j, where=dn):
+        return remote(ringout.at[g - 1, j], ringin.at[g - 1, j], rg_s.at[g - 1, j], rg_r.at[g - 1, j], where)
 
     def ring_in(g, j):
         return remote(ringout.at[g, j], ringin.at[g, j], rg_s.at[g, j], rg_r.at[g, j], up)
@@ -373,14 +409,14 @@
             @pl.when(block <= s)
             def _():
                 def write(gk, gv):
-                    mine[j, :, :HD] = gk
-                    mine[j, :, HD:] = gv
+                    mine[g, j, :, :HD] = gk
+                    mine[g, j, :, HD:] = gv
 
                 backward(block, write)
 
             @pl.when(block > s)
             def _():
-                mine[j] = jnp.zeros((TOK, 256), F32)
+                mine[g, j] = jnp.zeros((TOK, 256), F32)
 
             return carry
 
@@ -389,30 +425,36 @@
 
     def sum_up(g, j):
         sib_grad(g, j).wait_recv()
-        mine[j] += fromsib[g, j].astype(F32)
+        mine[g, j] += fromsib[g, j].astype(F32)
 
         @pl.when(up_needs(g))
         def _():
             ring_in(g, j).wait_recv()
-            mine[j] += ringin[g, j].astype(F32)
-
-    def backward_step(i, carry):
-        g = 5 - i
-
+            mine[g, j] += ringin[g, j].astype(F32)
+
+    def contribute(g):
         @pl.when(needed(z - g, z))
         def _():
             contributions(g)
+
+    def send_sum(g):
+        @pl.when(needed(z - g, z))
+        def _():
             for j in range(2):
                 sum_up(g, j)
-                ringout[g - 1, j] = mine[j].astype(BF)
-                ring_out(g, j).start()
-
-        return carry
-
-    lax.fori_loop(0, 5, backward_step, 0)
-    contributions(0)
-
-    def weight(n, act):
+                ringout[g - 1, j] = mine[g, j].astype(BF)
+                ring_out(g, j, near if g == 5 else dn).start()
+
+    contribute(5)
+    contribute(4)
+    send_sum(5)
+    contribute(3)
+    contribute(2)
+    send_sum(4)
+    contribute(1)
+    contribute(0)
+
+    def weight(n, act, lengths):
         grad = grads.at[n]
 
         def partial(t, j, core):
@@ -422,7 +464,7 @@
             return remote(wsib_out.at[n, t], wsib_in.at[n, t], ws_s.at[n, t], ws_r.at[n, t], sib)
 
         def target(k, way):
-            return lax.rem(z + 4 + k, 8) if way == 0 else lax.rem(z + 11 - k, 8)
+            return lax.rem(z + 8 - lengths[0] + k, 8) if way == 0 else lax.rem(z + 8 + lengths[1] - k, 8)
 
         def send_all():
             def one(i, carry):
@@ -434,46 +476,41 @@
 
             lax.fori_loop(0, 8, one, 0)
 
-        def hop(k, way):
+        def hop(k, way, j):
             out, into = (wd_out, wd_in) if way == 0 else (wu_out, wu_in)
             ss, rr = (wd_s, wd_r) if way == 0 else (wu_s, wu_r)
-            return remote(out.at[n, k], into.at[n, k], ss.at[n, k], rr.at[n, k], dn if way == 0 else up)
+            return remote(
+                out.at[n, k, j], into.at[n, k, j], ss.at[n, k, j], rr.at[n, k, j], dn if way == 0 else up
+            )
 
         def hop_step(k, way):
             out, into = (wd_out, wd_in) if way == 0 else (wu_out, wu_in)
             t = target(k, way)
             sib_copy(t).wait_recv()
             for j in range(2):
-                wacc[j] = partial(t, j, c) + wsib_in[n, t, j].astype(F32)
-
-            @pl.when(k > 0)
-            def _():
-                hop(k - 1, way).wait_recv()
-                for j in range(2):
-                    wacc[j] += into[n, k - 1, j].astype(F32)
-
-            for j in range(2):
-                out[n, k, j] = wacc[j].astype(BF)
-            hop(k, way).start()
+                total = partial(t, j, c) + wsib_in[n, t, j].astype(F32)
+                if k > 0:
+                    hop(k - 1, way, j).wait_recv()
+                    total += into[n, k - 1, j].astype(F32)
+                out[n, k, j] = total.astype(BF)
+                hop(k, way, j).start()
 
         def step(k):
-            hop_step(k, 0)
-
-            @pl.when(k < 3)
-            def _():
-                hop_step(k, 1)
+            for way in range(2):
+                if k < lengths[way]:
+                    hop_step(k, way)
 
         def x_copy():
             return remote(wx_out.at[n], wx_in.at[n], wx_s.at[n], wx_r.at[n], xp)
 
         def meet():
             sib_copy(z).wait_recv()
-            hop(3, 0).wait_recv()
-            hop(2, 1).wait_recv()
             for j in range(2):
+                for way in range(2):
+                    hop(lengths[way] - 1, way, j).wait_recv()
                 wacc[j] = (
                     partial(z, j, c) + wsib_in[n, z, j].astype(F32)
-                    + wd_in[n, 3, j].astype(F32) + wu_in[n, 2, j].astype(F32)
+                    + wd_in[n, lengths[0] - 1, j].astype(F32) + wu_in[n, lengths[1] - 1, j].astype(F32)
                 )
             wx_out[n] = wacc[1 - xh].astype(BF)
             x_copy().start()
@@ -482,39 +519,45 @@
         def drain():
             for t in range(8):
                 sib_copy(t).wait_send()
-            for k in range(4):
-                hop(k, 0).wait_send()
-            for k in range(3):
-                hop(k, 1).wait_send()
+            for way in range(2):
+                for k in range(lengths[way]):
+                    for j in range(2):
+                        hop(k, way, j).wait_send()
             x_copy().wait_send()
 
         return send_all, step, meet, x_copy, drain
 
-    wq = weight(0, anchor)
-    wkv = weight(1, projected)
+    wq = weight(0, anchor, (3, 4))
+    wkv = weight(1, projected, (4, 3))
     for h in range(2):
         grads[0, :, h * HD:(h + 1) * HD] = dq_t[:, h * TOK:(h + 1) * TOK].T.astype(BF)
+    send_sum(3)
     wq[0]()
+    send_sum(2)
     wq[1](0)
+    send_sum(1)
+    wq[1](1)
     for j in range(2):
         sum_up(0, j)
-    xout[...] = mine[1 - xh].astype(BF)
+
+        @pl.when(far_needs)
+        def _():
+            ring_in(4, j).wait_recv()
+            mine[0, j] += ringin[4, j].astype(F32)
+
+    xout[...] = mine[0, 1 - xh].astype(BF)
     x_rows = remote(xout, xin, xg_s, xg_r, xp)
     x_rows.start()
-    wq[1](1)
+    wq[1](2)
     x_rows.wait_recv()
-    grads[1] = (mine[xh] + xin[...].astype(F32)).astype(BF)
+    grads[1] = (mine[0, xh] + xin[...].astype(F32)).astype(BF)
+    wkv[0]()
+    wkv[1](0)
+    wq[1](3)
     for half in range(2):
         pairs[pl.ds(half, TOK, stride=2), :] = grads[1, :, half * HD:(half + 1) * HD].astype(F32)
     rows_ref[...] = pairs[:2 * TOK, :].astype(BF)
-    wkv[0]()
-
-    def both(k, carry):
-        wkv[1](k)
-        wq[1](k + 2)
-        return carry
-
-    lax.fori_loop(0, 2, both, 0)
+    wkv[1](1)
     own_q = wq[2]()
     gq_ref[...] = own_q
     wkv[1](2)
@@ -528,13 +571,20 @@
     for half in range(2):
         gkv_ref[pl.ds(half, 144, stride=2), :] = wacc[0, :, half * HD:(half + 1) * HD]
 
-    to_xp.wait_send()
+    for h in range(2):
+        to_xp(h).wait_send()
+        for j in range(2):
+            @pl.when(far_needs)
+            def _():
+                to_far(j, h).wait_send()
+
     x_rows.wait_send()
     wq[4]()
     wkv[4]()
     aug.drain()
     anc.drain()
-    pro.drain()
+    pros[0].drain()
+    pros[1].drain()
     for k in range(5):
         step(k).wait_send()
 
@@ -542,12 +592,13 @@
         @pl.when(needed(z - g, z))
         def _():
             for j in range(2):
-                to_sib(g, j).wait_send()
                 sib_grad(g, j).wait_send()
-
-                @pl.when(up_needs(g))
-                def _():
-                    to_up(g, j).wait_send()
+                for h in range(2):
+                    to_sib(g, j, h).wait_send()
+
+                    @pl.when(up_needs(g))
+                    def _():
+                        to_up(g, j, h).wait_send()
 
                 @pl.when(g > 0)
                 def _():
@@ -585,19 +636,19 @@
             pltpu.VMEM((HD, 512), F32), pltpu.VMEM((1, 512), F32),
             pltpu.VMEM((1, 512), jnp.int32), pltpu.VMEM((1, 512), jnp.int32),
             pltpu.VMEM((1, 512), F32), pltpu.VMEM((HD, 512), F32),
-            pltpu.VMEM((2, TOK, 256), F32),
+            pltpu.VMEM((6, 2, TOK, 256), F32),
             pltpu.VMEM((6, 2, TOK, 256), BF), pltpu.VMEM((6, 2, TOK, 256), BF),
             pltpu.VMEM((5, 2, TOK, 256), BF), pltpu.VMEM((5, 2, TOK, 256), BF),
             pltpu.VMEM((TOK, 256), BF), pltpu.VMEM((TOK, 256), BF),
             pltpu.VMEM((2, TOK, 256), BF),
             pltpu.VMEM((2, 8, 2, 144, 256), BF), pltpu.VMEM((2, 8, 2, 144, 256), BF),
             pltpu.VMEM((2, 4, 2, 144, 256), BF), pltpu.VMEM((2, 4, 2, 144, 256), BF),
-            pltpu.VMEM((2, 3, 2, 144, 256), BF), pltpu.VMEM((2, 3, 2, 144, 256), BF),
+            pltpu.VMEM((2, 4, 2, 144, 256), BF), pltpu.VMEM((2, 4, 2, 144, 256), BF),
             pltpu.VMEM((2, 144, 256), BF), pltpu.VMEM((2, 144, 256), BF),
             pltpu.VMEM((2, 144, 256), F32),
-            dma((3,)), *two((9,)), *two((9,)), *two((9,)), *two((5,)),
-            *two((5, 2)), *two((6, 2)), *two(()), *two((6, 2)), *two((5, 2)), *two(()),
-            *two((2, 8)), *two((2, 4)), *two((2, 3)), *two((2,)),
+            dma((3,)), *two((9,)), *two((9,)), *two((2, 9)), *two((5,)),
+            *two((5, 2, 2)), *two((6, 2, 2)), *two((2,)), *two((6, 2)), *two((5, 2)), *two(()),
+            *two((2, 8)), *two((2, 4, 2)), *two((2, 4, 2)), *two((2,)),
         ],
         compiler_params=pltpu.CompilerParams(
             collective_id=1, has_side_effects=True, vmem_limit_bytes=60 * 1024 * 1024

time: 164 us -> 162 us (0.988)
  Pallas kernels: 162 us -> 160 us
    pallas_call x1, Pallas kernels: 160 us -> 158 us  [step_call(): pl.pallas_call(step_kernel, out_shape=[jax.ShapeDtypeStruct((TOK, 256), B...]
where the time goes in v3:
time: 162 us; the launch traced here: 161 us
  Pallas kernels  160 us (99%)
    pallas_call x1, Pallas kernels, step_call(): pl.pallas_call(step_kernel, out_shape=[jax.ShapeDtypeStruct((TOK, 256), B...  158 us

profile of v3, /device:TPU:8, one launch (start us, length us, event | category | flops | bytes accessed | tf_op | source)
XLA Modules:
  0.0 161.0 jit_solution(2036335935318782054)
XLA Ops:
  0.6 158.4 %shard_map.102 = (bf16[256,256]{1,0:T(8,128)(2,1)}, f32[144,256]{1,0:T(8,128)}, f32[288,128]{1,0:T(8,128)}, bf16[512,128]{1,0:T(8,128)(2,1)}) custom-call(bf16[288,256]{1,0:T(8,128)(2,1)} %bitcast.14, bf16[576,256]{1,0:T(8,128)(2,1)} %bitcast.13, bf16[576,2304]{1,0:T(8,128)(2,1)} %bitcast.11, bf16[4608,256]{1,0:T(8,128)(2,1)} %qw_hbm.1, ...), custom_call_target="tpu_custom_call" | custom-call | tf_op jit(solution)/shard_map/pallas_call | solution.py:617
  159.1 1.9 %shard_map.103 = (bf16[256,256]{1,0:T(8,128)(2,1)}, f32[144,256]{1,0:T(8,128)}, f32[288,128]{1,0:T(8,128)}, bf16[512,128]{1,0:T(8,128)(2,1)}) custom-call(bf16[256,256]{1,0:T(8,128)(2,1)} %get-tuple-element.12.refs_0_, f32[144,256]{1,0:T(8,128)} %get-tuple-element.13.refs_1_, f32[288,128]{1,0:T(8,128)} %get-tuple-element.14.refs_2_, ...), custom_call_target="tpu_custom_call" | custom-call | tf_op jit(solution)/shard_map/pallas_call | solution.py:670

commit v4 on v3

--- a/solution.py
+++ b/solution.py
@@ -45,80 +45,64 @@
 class FeatureGather:
     def __init__(self, own, buf, rows, send, recv, m, lanes=pl.ds(0, TOK)):
         self.own, self.buf, self.rows, self.send, self.recv = own, buf, rows, send, recv
-        self.lanes = lanes
-        self.m = m
+        self.lanes, self.m = lanes, m
         self.p = m + 1 - 2 * lax.rem(m, 2)
         self.up, self.dn = lax.rem(m + 2, 8), lax.rem(m + 6, 8)
-
-    def part(self, block, half=None):
-        n = self.rows if half is None else self.rows // 2
-        start = block * self.rows + (half or 0) * n
-        return self.buf.at[pl.ds(pl.multiple_of(start, 16), n), self.lanes]
-
-    def copy(self, i, src, dst, to):
+        self.o = lax.rem(m + 4, 8)
+        p = self.p
+        self.p_up, self.p_dn, self.p_o = lax.rem(p + 2, 8), lax.rem(p + 6, 8), lax.rem(p + 4, 8)
+        n = rows // 9
+        whole, left, right = (0, 9 * n), (0, 5 * n), (5 * n, 4 * n)
+        top, bottom = (0, rows // 2), (rows // 2, rows // 2)
+        left0, left1 = (0, 5 * n // 2), (5 * n // 2, 5 * n // 2)
+        m, p, up, dn = self.m, self.p, self.up, self.dn
+        self.out = [
+            (m, left, p), (m, whole, up), (m, whole, dn), (p, left, up), (p, left, dn),
+            (dn, top, up), (up, bottom, dn), (self.p_dn, left0, up), (self.p_up, left1, dn),
+            (m, right, p), (dn, right, p), (up, right, p), (self.o, right, p),
+        ]
+        self.into = [
+            (p, left), (dn, whole), (up, whole), (self.p_dn, left), (self.p_up, left),
+            (self.o, top), (self.o, bottom), (self.p_o, left0), (self.p_o, left1),
+            (p, right), (self.p_dn, right), (self.p_up, right), (self.p_o, right),
+        ]
+
+    def part(self, block, rows):
+        start = block * self.rows + rows[0]
+        return self.buf.at[pl.ds(pl.multiple_of(start, 16), rows[1]), self.lanes]
+
+    def sent(self, i):
+        block, rows, to = self.out[i]
+        dst = self.part(block, rows)
+        src = self.own.at[pl.ds(*rows)] if i in (0, 1, 2, 9) else dst
         return remote(src, dst, self.send.at[i], self.recv.at[i], {"mp": to})
 
-    def sent(self, i):
-        m, p = self.m, self.p
-        a, b = lax.rem(m + 6, 8), lax.rem(m + 2, 8)
-        pa, pb = lax.rem(p + 6, 8), lax.rem(p + 2, 8)
-        table = [
-            (m, None, p), (m, None, self.up), (m, None, self.dn),
-            (p, None, self.up), (p, None, self.dn),
-            (a, 0, self.up), (b, 1, self.dn),
-            (pa, 0, self.up), (pb, 1, self.dn),
-        ]
-        block, half, to = table[i]
-        dst = self.part(block, half)
-        return self.copy(i, self.own if i < 3 else dst, dst, to)
-
     def arrived(self, i):
-        m, p = self.m, self.p
-        o, po = lax.rem(m + 4, 8), lax.rem(p + 4, 8)
-        table = [
-            (p, None), (self.dn, None), (self.up, None),
-            (lax.rem(p + 6, 8), None), (lax.rem(p + 2, 8), None),
-            (o, 0), (o, 1), (po, 0), (po, 1),
-        ]
-        block, half = table[i]
-        dst = self.part(block, half)
-        return self.copy(i, dst, dst, p)
+        dst = self.part(*self.into[i])
+        return remote(dst, dst, self.send.at[i], self.recv.at[i], {"mp": self.p})
 
     def start(self):
-        for i in range(3):
+        for i in (0, 1, 2, 9):
             self.sent(i).start()
 
     def relay(self, stage):
-        if stage == 0:
-            self.arrived(0).wait_recv()
-            self.sent(3).start()
-            self.sent(4).start()
-        elif stage == 1:
-            self.arrived(1).wait_recv()
-            self.sent(5).start()
-            self.arrived(2).wait_recv()
-            self.sent(6).start()
-        elif stage == 2:
-            self.arrived(3).wait_recv()
-            self.sent(7).start()
-            self.arrived(4).wait_recv()
-            self.sent(8).start()
-        elif stage == 3:
-            self.arrived(5).wait_recv()
-            self.arrived(6).wait_recv()
-        else:
-            self.arrived(7).wait_recv()
-            self.arrived(8).wait_recv()
+        waits, sends = [
+            ((0,), (3, 4)), ((1,), (5, 10)), ((2,), (6, 11)), ((3,), (7,)), ((4,), (8,)),
+            ((6,), (12,)), ((5,), ()), ((9, 10, 11), ()), ((7, 8, 12), ()),
+        ][stage]
+        for i in waits:
+            self.arrived(i).wait_recv()
+        for i in sends:
+            self.sent(i).start()
 
     def blocks(self, stage):
-        m, p = self.m, self.p
-        return [
-            [p], [self.dn, self.up], [lax.rem(p + 6, 8), lax.rem(p + 2, 8)],
-            [lax.rem(m + 4, 8)], [lax.rem(p + 4, 8)],
-        ][stage]
+        return {
+            1: [self.dn], 2: [self.up], 6: [self.o],
+            7: [self.p, self.p_dn, self.p_up], 8: [self.p_o],
+        }.get(stage, [])
 
     def drain(self):
-        for i in range(9):
+        for i in range(13):
             self.sent(i).wait_send()
 
 
@@ -162,9 +146,11 @@
         for h, half in enumerate(halves)
     ]
     far, near = {"seq": lax.rem(s + 20, 32)}, {"seq": lax.rem(s + 12, 32)}
+    across = 2 - 4 * xh
+    ring = [up, dn, far, near]
     greet(
-        [{"mp": aug.p}, {"mp": aug.up}, {"mp": aug.dn}, up, dn, far, near]
-        + [{"seq": h} for h in hyper]
+        [{"mp": aug.p}, {"mp": aug.up}, {"mp": aug.dn}] + ring
+        + [{"seq": one["seq"] + across} for one in ring] + [{"seq": h} for h in hyper]
     )
 
     aug.start()
@@ -193,10 +179,13 @@
             kw[pl.ds(pl.multiple_of(i * 576, 576), 576), half * HD:(half + 1) * HD] = out
         return carry
 
-    for stage in range(5):
+    for stage in range(9):
         aug.relay(stage)
-        count(stage)
-        lax.fori_loop(2 * stage, min(2 * stage + 2, 8), unpair, 0)
+        if stage < 5:
+            count(stage)
+            lax.fori_loop(2 * stage, min(2 * stage + 2, 8), unpair, 0)
+        if stage == 5:
+            anc.start()
     here = doc * cnt_out[5, 0:1, 0:1]
     lanes = lax.broadcasted_iota(jnp.int32, (1, 2 * TOK), 1)
     place[...] = lax.rem(lanes, TOK) + s * TOK
@@ -290,14 +279,14 @@
     acc[...] = jnp.zeros_like(acc)
     for h in range(2):
         add_kv(h, m)
-        for stage in range(5):
+        for stage in range(9):
             pros[h].relay(stage)
-            if stage == 2:
-                if h == 0:
-                    pros[1].start()
-                else:
-                    anc.start()
-                    second(0)
+            if stage == 4 and h == 0:
+                pros[1].start()
+            if stage == 5 and h == 1:
+                second(0)
+                for early in range(3):
+                    anc.relay(early)
             for block in pros[h].blocks(stage):
                 add_kv(h, block)
         launch(h)
@@ -330,12 +319,13 @@
 
     acc[...] = jnp.zeros_like(acc)
     add(m)
-    for stage in range(5):
-        anc.relay(stage)
+    for stage in range(9):
+        if stage > 2:
+            anc.relay(stage)
         for block in anc.blocks(stage):
             add(block)
-        if stage < 3:
-            pass_on((stage + 3) // 2, (stage + 1) % 2)
+        if stage in (4, 5, 6):
+            pass_on((stage - 1) // 2, (stage + 1) % 2)
 
     query = acc[...].astype(BF)
     for h in range(2):
@@ -367,11 +357,18 @@
     for h in range(2):
         att_ref[:, h * HD:(h + 1) * HD] = attended[:, h * TOK:(h + 1) * TOK].T
 
-    def ring_out(g, j, where=dn):
-        return remote(ringout.at[g - 1, j], ringin.at[g - 1, j], rg_s.at[g - 1, j], rg_r.at[g - 1, j], where)
-
-    def ring_in(g, j):
-        return remote(ringout.at[g, j], ringin.at[g, j], rg_s.at[g, j], rg_r.at[g, j], up)
+    def piece(k):
+        return lax.rem(xh + k, 2)
+
+    def there(where, k):
+        return {"seq": where["seq"] + k * across}
+
+    def ring_out(g, k, last=False):
+        where = there(near if g == 5 else dn, k) if last else dn
+        return remote(ringout.at[g - 1, k], ringin.at[g - 1, k], rg_s.at[g - 1, k], rg_r.at[g - 1, k], where)
+
+    def ring_in(g, k):
+        return remote(ringout.at[g, k], ringin.at[g, k], rg_s.at[g, k], rg_r.at[g, k], up)
 
     def sib_grad(g, j):
         return remote(tosib.at[g, j], fromsib.at[g, j], gs_s.at[g, j], gs_r.at[g, j], sib)
@@ -423,15 +420,6 @@
         lax.fori_loop(0, 2, for_sib, 0)
         lax.fori_loop(0, 2, for_me, 0)
 
-    def sum_up(g, j):
-        sib_grad(g, j).wait_recv()
-        mine[g, j] += fromsib[g, j].astype(F32)
-
-        @pl.when(up_needs(g))
-        def _():
-            ring_in(g, j).wait_recv()
-            mine[g, j] += ringin[g, j].astype(F32)
-
     def contribute(g):
         @pl.when(needed(z - g, z))
         def _():
@@ -440,18 +428,29 @@
     def send_sum(g):
         @pl.when(needed(z - g, z))
         def _():
-            for j in range(2):
-                sum_up(g, j)
-                ringout[g - 1, j] = mine[g, j].astype(BF)
-                ring_out(g, j, near if g == 5 else dn).start()
-
+            for k in (1, 0):
+                j = piece(k)
+                sib_grad(g, j).wait_recv()
+                mine[g, j] += fromsib[g, j].astype(F32)
+
+                @pl.when(up_needs(g))
+                def _():
+                    ring_in(g, k).wait_recv()
+                    mine[g, j] += ringin[g, k].astype(F32)
+
+                ringout[g - 1, k] = mine[g, j].astype(BF)
+                ring_out(g, k, g in (1, 5)).start()
+
+    contribute(4)
+    send_sum(4)
+    contribute(3)
     contribute(5)
-    contribute(4)
     send_sum(5)
-    contribute(3)
+    send_sum(3)
     contribute(2)
-    send_sum(4)
+    send_sum(2)
     contribute(1)
+    send_sum(1)
     contribute(0)
 
     def weight(n, act, lengths):
@@ -466,34 +465,34 @@
         def target(k, way):
             return lax.rem(z + 8 - lengths[0] + k, 8) if way == 0 else lax.rem(z + 8 + lengths[1] - k, 8)
 
-        def send_all():
-            def one(i, carry):
-                t = lax.rem(z + 4 + 7 * lax.rem(i, 2) * (i // 2 + 1) + (1 - lax.rem(i, 2)) * (i // 2), 8)
+        def push(*targets):
+            for t in targets:
                 for j in range(2):
                     wsib_out[n, t, j] = partial(t, j, 1 - c).astype(BF)
                 sib_copy(t).start()
-                return carry
-
-            lax.fori_loop(0, 8, one, 0)
-
-        def hop(k, way, j):
+
+        def push_for(k):
+            push(*[target(k, way) for way in range(2) if k < lengths[way]])
+
+        def hop(k, way, q):
             out, into = (wd_out, wd_in) if way == 0 else (wu_out, wu_in)
             ss, rr = (wd_s, wd_r) if way == 0 else (wu_s, wu_r)
-            return remote(
-                out.at[n, k, j], into.at[n, k, j], ss.at[n, k, j], rr.at[n, k, j], dn if way == 0 else up
-            )
+            where = dn if way == 0 else up
+            if k == lengths[way] - 1:
+                where = there(where, q)
+            return remote(out.at[n, k, q], into.at[n, k, q], ss.at[n, k, q], rr.at[n, k, q], where)
 
         def hop_step(k, way):
             out, into = (wd_out, wd_in) if way == 0 else (wu_out, wu_in)
             t = target(k, way)
             sib_copy(t).wait_recv()
-            for j in range(2):
-                total = partial(t, j, c) + wsib_in[n, t, j].astype(F32)
+            for q in (1, 0):
+                total = partial(t, piece(q), c) + wsib_in[n, t, piece(q)].astype(F32)
                 if k > 0:
-                    hop(k - 1, way, j).wait_recv()
-                    total += into[n, k - 1, j].astype(F32)
-                out[n, k, j] = total.astype(BF)
-                hop(k, way, j).start()
+                    hop(k - 1, way, q).wait_recv()
+                    total += into[n, k - 1, q].astype(F32)
+                out[n, k, q] = total.astype(BF)
+                hop(k, way, q).start()
 
         def step(k):
             for way in range(2):
@@ -503,73 +502,87 @@
         def x_copy():
             return remote(wx_out.at[n], wx_in.at[n], wx_s.at[n], wx_r.at[n], xp)
 
+        def cross():
+            sib_copy(z).wait_recv()
+            for q in (1, 0):
+                wacc[n, q] = partial(z, piece(q), c) + wsib_in[n, z, piece(q)].astype(F32)
+            wx_out[n] = wacc[n, 1].astype(BF)
+            x_copy().start()
+
         def meet():
-            sib_copy(z).wait_recv()
-            for j in range(2):
-                for way in range(2):
-                    hop(lengths[way] - 1, way, j).wait_recv()
-                wacc[j] = (
-                    partial(z, j, c) + wsib_in[n, z, j].astype(F32)
-                    + wd_in[n, lengths[0] - 1, j].astype(F32) + wu_in[n, lengths[1] - 1, j].astype(F32)
-                )
-            wx_out[n] = wacc[1 - xh].astype(BF)
-            x_copy().start()
-            return wacc[xh]
+            x_copy().wait_recv()
+            total = wacc[n, 0] + wx_in[n].astype(F32)
+            for way, into in enumerate((wd_in, wu_in)):
+                for q in range(2):
+                    hop(lengths[way] - 1, way, q).wait_recv()
+                    total += into[n, lengths[way] - 1, q].astype(F32)
+            return total
 
         def drain():
             for t in range(8):
                 sib_copy(t).wait_send()
             for way in range(2):
                 for k in range(lengths[way]):
-                    for j in range(2):
-                        hop(k, way, j).wait_send()
+                    for q in range(2):
+                        hop(k, way, q).wait_send()
             x_copy().wait_send()
 
-        return send_all, step, meet, x_copy, drain
-
-    wq = weight(0, anchor, (3, 4))
-    wkv = weight(1, projected, (4, 3))
+        return push, push_for, step, cross, meet, drain
+
+    push_q, push_q_for, step_q, cross_q, meet_q, drain_q = weight(0, anchor, (3, 4))
+    push_kv, push_kv_for, step_kv, cross_kv, meet_kv, drain_kv = weight(1, projected, (4, 3))
+    for k in (1, 0):
+        sib_grad(0, piece(k)).wait_recv()
+        mine[0, piece(k)] += fromsib[0, piece(k)].astype(F32)
+        if k == 1:
+            xout[...] = mine[0, piece(1)].astype(BF)
+            x_rows = remote(xout, xin, xg_s, xg_r, xp)
+            x_rows.start()
     for h in range(2):
         grads[0, :, h * HD:(h + 1) * HD] = dq_t[:, h * TOK:(h + 1) * TOK].T.astype(BF)
-    send_sum(3)
-    wq[0]()
-    send_sum(2)
-    wq[1](0)
-    send_sum(1)
-    wq[1](1)
-    for j in range(2):
-        sum_up(0, j)
-
+    push_q_for(0)
+    push_q_for(1)
+    step_q(0)
+    push_q_for(2)
+    push_q_for(3)
+    push_q(z)
+    x_rows.wait_recv()
+    own = mine[0, xh] + xin[...].astype(F32)
+    mine[0, xh] = own
+    for k in range(2):
         @pl.when(far_needs)
         def _():
-            ring_in(4, j).wait_recv()
-            mine[0, j] += ringin[4, j].astype(F32)
-
-    xout[...] = mine[0, 1 - xh].astype(BF)
-    x_rows = remote(xout, xin, xg_s, xg_r, xp)
-    x_rows.start()
-    wq[1](2)
-    x_rows.wait_recv()
-    grads[1] = (mine[0, xh] + xin[...].astype(F32)).astype(BF)
-    wkv[0]()
-    wkv[1](0)
-    wq[1](3)
+            ring_in(4, k).wait_recv()
+            mine[0, xh] += ringin[4, k].astype(F32)
+
+    for k in range(2):
+        @pl.when(up_needs(0))
+        def _():
+            ring_in(0, k).wait_recv()
+            mine[0, xh] += ringin[0, k].astype(F32)
+
+    grads[1] = mine[0, xh].astype(BF)
+    push_kv_for(0)
+    push_kv_for(1)
+    step_kv(0)
+    step_q(1)
+    push_kv_for(2)
+    step_kv(1)
+    step_q(2)
+    push_kv_for(3)
+    push_kv(z)
+    step_kv(2)
+    cross_kv()
+    cross_q()
+    step_kv(3)
+    step_q(3)
     for half in range(2):
         pairs[pl.ds(half, TOK, stride=2), :] = grads[1, :, half * HD:(half + 1) * HD].astype(F32)
     rows_ref[...] = pairs[:2 * TOK, :].astype(BF)
-    wkv[1](1)
-    own_q = wq[2]()
-    gq_ref[...] = own_q
-    wkv[1](2)
-    wkv[1](3)
-    own_kv = wkv[2]()
-    wacc[0] = own_kv
-    wq[3]().wait_recv()
-    gq_ref[...] += wx_in[0].astype(F32)
-    wkv[3]().wait_recv()
-    wacc[0] += wx_in[1].astype(F32)
+    gq_ref[...] = meet_q()
+    wacc[1, 0] = meet_kv()
     for half in range(2):
-        gkv_ref[pl.ds(half, 144, stride=2), :] = wacc[0, :, half * HD:(half + 1) * HD]
+        gkv_ref[pl.ds(half, 144, stride=2), :] = wacc[1, 0, :, half * HD:(half + 1) * HD]
 
     for h in range(2):
         to_xp(h).wait_send()
@@ -579,8 +592,8 @@
                 to_far(j, h).wait_send()
 
     x_rows.wait_send()
-    wq[4]()
-    wkv[4]()
+    drain_q()
+    drain_kv()
     aug.drain()
     anc.drain()
     pros[0].drain()
@@ -645,8 +658,8 @@
             pltpu.VMEM((2, 4, 2, 144, 256), BF), pltpu.VMEM((2, 4, 2, 144, 256), BF),
             pltpu.VMEM((2, 4, 2, 144, 256), BF), pltpu.VMEM((2, 4, 2, 144, 256), BF),
             pltpu.VMEM((2, 144, 256), BF), pltpu.VMEM((2, 144, 256), BF),
-            pltpu.VMEM((2, 144, 256), F32),
-            dma((3,)), *two((9,)), *two((9,)), *two((2, 9)), *two((5,)),
+            pltpu.VMEM((2, 2, 144, 256), F32),
+            dma((3,)), *two((13,)), *two((13,)), *two((2, 13)), *two((5,)),
             *two((5, 2, 2)), *two((6, 2, 2)), *two((2,)), *two((6, 2)), *two((5, 2)), *two(()),
             *two((2, 8)), *two((2, 4, 2)), *two((2, 4, 2)), *two((2,)),
         ],

time: 162 us -> 147 us (0.907)
  Pallas kernels: 160 us -> 145 us
    pallas_call x1, Pallas kernels: 158 us -> 143 us  [step_call(): pl.pallas_call(step_kernel, out_shape=[jax.ShapeDtypeStruct((TOK, 256), B...]
where the time goes in v4:
time: 147 us; the launch traced here: 146 us
  Pallas kernels  145 us (99%)
    pallas_call x1, Pallas kernels, step_call(): pl.pallas_call(step_kernel, out_shape=[jax.ShapeDtypeStruct((TOK, 256), B...  143 us

profile of v4, /device:TPU:8, one launch (start us, length us, event | category | flops | bytes accessed | tf_op | source)
XLA Modules:
  0.0 145.8 jit_solution(6043194724804050907)
XLA Ops:
  0.6 143.3 %shard_map.102 = (bf16[256,256]{1,0:T(8,128)(2,1)}, f32[144,256]{1,0:T(8,128)}, f32[288,128]{1,0:T(8,128)}, bf16[512,128]{1,0:T(8,128)(2,1)}) custom-call(bf16[288,256]{1,0:T(8,128)(2,1)} %bitcast.14, bf16[576,256]{1,0:T(8,128)(2,1)} %bitcast.13, bf16[576,2304]{1,0:T(8,128)(2,1)} %bitcast.11, bf16[4608,256]{1,0:T(8,128)(2,1)} %qw_hbm.1, ...), custom_call_target="tpu_custom_call" | custom-call | tf_op jit(solution)/shard_map/pallas_call | solution.py:630
  143.9 1.9 %shard_map.103 = (bf16[256,256]{1,0:T(8,128)(2,1)}, f32[144,256]{1,0:T(8,128)}, f32[288,128]{1,0:T(8,128)}, bf16[512,128]{1,0:T(8,128)(2,1)}) custom-call(bf16[256,256]{1,0:T(8,128)(2,1)} %get-tuple-element.12.refs_0_, f32[144,256]{1,0:T(8,128)} %get-tuple-element.13.refs_1_, f32[288,128]{1,0:T(8,128)} %get-tuple-element.14.refs_2_, ...), custom_call_target="tpu_custom_call" | custom-call | tf_op jit(solution)/shard_map/pallas_call | solution.py:683

commit v5 on v4

--- a/solution.py
+++ b/solution.py
@@ -150,7 +150,7 @@
     ring = [up, dn, far, near]
     greet(
         [{"mp": aug.p}, {"mp": aug.up}, {"mp": aug.dn}] + ring
-        + [{"seq": one["seq"] + across} for one in ring] + [{"seq": h} for h in hyper]
+        + [{"seq": one["seq"] + across} for one in ring[:2]] + [{"seq": h} for h in hyper]
     )
 
     aug.start()
@@ -179,28 +179,25 @@
             kw[pl.ds(pl.multiple_of(i * 576, 576), 576), half * HD:(half + 1) * HD] = out
         return carry
 
-    for stage in range(9):
-        aug.relay(stage)
-        if stage < 5:
-            count(stage)
-            lax.fori_loop(2 * stage, min(2 * stage + 2, 8), unpair, 0)
-        if stage == 5:
-            anc.start()
-    here = doc * cnt_out[5, 0:1, 0:1]
+    lax.fori_loop(0, 2, unpair, 0)
     lanes = lax.broadcasted_iota(jnp.int32, (1, 2 * TOK), 1)
     place[...] = lax.rem(lanes, TOK) + s * TOK
     for h in range(2):
         cut = slice(h * TOK, (h + 1) * TOK)
         head = slice(h * HD, (h + 1) * HD)
-        first[:, cut] = here
         do_n[cut, :] = dout_ref[:, head]
         do_t[:, cut] = dout_ref[:, head].T
     loads[0].wait()
     loads[1].wait()
-    for h, half in enumerate(halves):
-        own_projected[:, half] = dot(pw[...], augment[:, half]).astype(BF)
-        if h == 0:
-            pros[0].start()
+    for stage in range(9):
+        aug.relay(stage)
+        if stage == 4:
+            anc.start()
+            lax.fori_loop(2, 6, unpair, 0)
+    own_projected[...] = dot(pw[...], augment[...]).astype(BF)
+    pros[0].start()
+    count(0)
+    lax.fori_loop(6, 8, unpair, 0)
 
     def add(block):
         acc[...] += dot_tn(rows_of(anchor, block * 576, 576)[...], rows_of(qw, block * 576, 576)[...])
@@ -216,85 +213,106 @@
     def lane(t, j):
         return 4 * t + 2 * j + c
 
-    def to_up(g, j, h, src=None):
-        return half_copy(src, lane(z - g, j), h, up_s.at[g, j, h], up_r.at[g, j, h], up)
-
-    def to_far(j, h, src=None):
-        return half_copy(src, lane(z, j), h, up_s.at[4, j, h], up_r.at[4, j, h], far)
-
-    def to_sib(g, j, h, src=None):
-        return half_copy(src, lane(z - g, j), h, sb_s.at[g, j, h], sb_r.at[g, j, h], sib)
-
-    def from_sib(g, j, h):
-        b = 4 * (z - g) + 2 * j + 1 - c
-        return half_copy(None, b, h, sb_s.at[g, j, h], sb_r.at[g, j, h], sib)
-
-    def from_dn(g, j, h):
-        return half_copy(None, lane(z - g, j), h, up_s.at[g - 1, j, h], up_r.at[g - 1, j, h], dn)
+    def piece(k):
+        return lax.rem(xh + k, 2)
+
+    def to_up(g, h, src=None):
+        return half_copy(src, lane(z - g, xh), h, up_s.at[g, h], up_r.at[g, h], up)
+
+    def to_far(h, src=None):
+        return half_copy(src, lane(z, xh), h, up_s.at[4, h], up_r.at[4, h], far)
+
+    def to_xp(g, h, src=None):
+        return half_copy(src, lane(z - g, xh), h, xp_s.at[g, h], xp_r.at[g, h], xp)
+
+    def to_sib(g, k, h, src=None):
+        return half_copy(src, lane(z - g, piece(k)), h, sb_s.at[g, k, h], sb_r.at[g, k, h], sib)
+
+    def from_sib(g, k, h):
+        b = 4 * (z - g) + 2 * piece(k) + 1 - c
+        return half_copy(None, b, h, sb_s.at[g, k, h], sb_r.at[g, k, h], sib)
+
+    def from_dn(g, h):
+        return half_copy(None, lane(z - g, xh), h, up_s.at[g - 1, h], up_r.at[g - 1, h], dn)
+
+    def from_xp(g, h):
+        return half_copy(None, lane(z - g, 1 - xh), h, xp_s.at[g, h], xp_r.at[g, h], xp)
 
     def up_needs(g):
         return (g < 4) & needed(z - g, z + 1)
 
     far_needs = needed(z, z + 5)
 
-    def to_xp(h):
-        return half_copy(kv_ref, s, h, xp_s.at[h], xp_r.at[h], xp)
-
-    def from_xp(h):
-        return half_copy(None, xp_id, h, xp_s.at[h], xp_r.at[h], xp)
-
-    def spread(j, h, src=None):
-        @pl.when(up_needs(0))
-        def _():
-            to_up(0, j, h, src).start()
-
-        @pl.when(far_needs)
-        def _():
-            to_far(j, h, src).start()
-
-        to_sib(0, j, h, src).start()
-
     def launch(h):
         kv_ref[halves[h]] = acc[halves[h]].astype(BF)
-        to_xp(h).start()
-        spread(xh, h, kv_ref)
+
+        @pl.when(up_needs(0))
+        def _():
+            to_up(0, h, kv_ref).start()
+
+        to_xp(0, h, kv_ref).start()
+        to_sib(0, 0, h, kv_ref).start()
+
+        @pl.when(far_needs)
+        def _():
+            to_far(h, kv_ref).start()
+
         kvs[s, halves[h]] = kv_ref[halves[h]]
-
-    def second(h):
-        from_xp(h).wait_recv()
-        spread(1 - xh, h)
 
     def pass_on(g, h):
         @pl.when(needed(z - g, z))
         def _():
-            for j in range(2):
-                from_dn(g, j, h).wait_recv()
-
-                @pl.when(up_needs(g))
-                def _():
-                    to_up(g, j, h).start()
-
-                to_sib(g, j, h).start()
+            from_dn(g, h).wait_recv()
+
+            @pl.when(up_needs(g))
+            def _():
+                to_up(g, h).start()
+
+            to_xp(g, h).start()
+            to_sib(g, 0, h).start()
+
+    def crossed(g, h):
+        @pl.when(needed(z - g, z))
+        def _():
+            from_xp(g, h).wait_recv()
+            to_sib(g, 1, h).start()
 
     acc[...] = jnp.zeros_like(acc)
-    for h in range(2):
-        add_kv(h, m)
-        for stage in range(9):
+    def gather(h, *stages):
+        for stage in stages:
             pros[h].relay(stage)
-            if stage == 4 and h == 0:
-                pros[1].start()
-            if stage == 5 and h == 1:
-                second(0)
-                for early in range(3):
-                    anc.relay(early)
             for block in pros[h].blocks(stage):
                 add_kv(h, block)
-        launch(h)
+
+    add_kv(0, m)
+    gather(0, 0, 1, 2, 3, 4)
+    pros[1].start()
+    for stage in range(3):
+        anc.relay(stage)
+    count(1)
+    add_kv(1, m)
+    gather(0, 5, 6, 7)
+    pros[1].relay(0)
+    gather(0, 8)
+    launch(0)
+    count(2)
+    gather(1, 1, 2, 3, 4)
     pass_on(1, 0)
+    for stage in range(3, 6):
+        anc.relay(stage)
+    count(3)
+    gather(1, 5, 6)
+    pass_on(2, 0)
+    gather(1, 7, 8)
+    launch(1)
+    pass_on(3, 0)
+    count(4)
+    for h in range(2):
+        first[:, h * TOK:(h + 1) * TOK] = doc * cnt_out[5, 0:1, 0:1]
     num[...] = jnp.zeros_like(num)
     den[...] = jnp.zeros_like(den)
     dq_t[...] = jnp.zeros_like(dq_t)
-    second(1)
+    crossed(0, 0)
 
     def scores(block):
         k, v = kvs[block, :, :HD], kvs[block, :, HD:]
@@ -318,14 +336,16 @@
         lax.fori_loop(0, 4, one, 0)
 
     acc[...] = jnp.zeros_like(acc)
-    add(m)
-    for stage in range(9):
-        if stage > 2:
-            anc.relay(stage)
+    for block in (m, anc.dn, anc.up):
+        add(block)
+    for stage in range(6, 9):
+        anc.relay(stage)
         for block in anc.blocks(stage):
             add(block)
-        if stage in (4, 5, 6):
-            pass_on((stage - 1) // 2, (stage + 1) % 2)
+    pass_on(1, 1)
+    pass_on(4, 0)
+    crossed(1, 0)
+    crossed(0, 1)
 
     query = acc[...].astype(BF)
     for h in range(2):
@@ -334,22 +354,33 @@
         q_n[cut, :] = query[:, head]
         q_t[:, cut] = query[:, head].T
 
-    def forward_step(g, carry):
+    def forward_step(g):
         @pl.when(needed(z - g, z))
         def _():
-            @pl.when(g > 2)
-            def _():
-                for h in range(2):
-                    pass_on(g, h)
-
             for h in range(2):
-                for j in range(2):
-                    from_sib(g, j, h).wait_recv()
+                for k in range(2):
+                    from_sib(g, k, h).wait_recv()
             forward(g)
 
-        return carry
-
-    lax.fori_loop(0, 6, forward_step, 0)
+    pass_on(2, 1)
+    crossed(1, 1)
+    forward_step(0)
+    pass_on(3, 1)
+    crossed(2, 0)
+    crossed(2, 1)
+    forward_step(1)
+    pass_on(4, 1)
+    crossed(3, 0)
+    crossed(3, 1)
+    pass_on(5, 0)
+    pass_on(5, 1)
+    forward_step(2)
+    for g in (4, 5):
+        for h in range(2):
+            crossed(g, h)
+    forward_step(3)
+    forward_step(5)
+    forward_step(4)
 
     attended = (num[...] * (1.0 / den[...])).astype(BF)
     delta[...] = jnp.sum(do_t[...].astype(F32) * attended.astype(F32), axis=0, keepdims=True)
@@ -357,21 +388,20 @@
     for h in range(2):
         att_ref[:, h * HD:(h + 1) * HD] = attended[:, h * TOK:(h + 1) * TOK].T
 
-    def piece(k):
-        return lax.rem(xh + k, 2)
-
     def there(where, k):
         return {"seq": where["seq"] + k * across}
 
-    def ring_out(g, k, last=False):
-        where = there(near if g == 5 else dn, k) if last else dn
-        return remote(ringout.at[g - 1, k], ringin.at[g - 1, k], rg_s.at[g - 1, k], rg_r.at[g - 1, k], where)
-
-    def ring_in(g, k):
-        return remote(ringout.at[g, k], ringin.at[g, k], rg_s.at[g, k], rg_r.at[g, k], up)
-
-    def sib_grad(g, j):
-        return remote(tosib.at[g, j], fromsib.at[g, j], gs_s.at[g, j], gs_r.at[g, j], sib)
+    def ring_out(g, h, where=dn):
+        return remote(ringout.at[g - 1, h], ringin.at[g - 1, h], rg_s.at[g - 1, h], rg_r.at[g - 1, h], where)
+
+    def ring_in(g, h):
+        return remote(ringout.at[g, h], ringin.at[g, h], rg_s.at[g, h], rg_r.at[g, h], up)
+
+    def sib_grad(g, k):
+        return remote(tosib.at[g, k], fromsib.at[g, k], gs_s.at[g, k], gs_r.at[g, k], sib)
+
+    def x_grad(g, h):
+        return remote(xout.at[g, h], xin.at[g, h], xg_s.at[g, h], xg_r.at[g, h], xp)
 
     def backward(block, write):
         k, v, th, w = scores(block)
@@ -382,38 +412,47 @@
         dq_t[...] += dot_tn(k, raw)
 
     def contributions(g):
-        def for_sib(j, carry):
-            block = 4 * (z - g) + 2 * j + 1 - c
+        def for_sib(i, carry):
+            k = 1 - i
+            block = 4 * (z - g) + 2 * piece(k) + 1 - c
 
             @pl.when(block <= s)
             def _():
                 def write(gk, gv):
-                    tosib[g, j, :, :HD] = gk.astype(BF)
-                    tosib[g, j, :, HD:] = gv.astype(BF)
+                    tosib[g, k, :, :HD] = gk.astype(BF)
+                    tosib[g, k, :, HD:] = gv.astype(BF)
 
                 backward(block, write)
 
             @pl.when(block > s)
             def _():
-                tosib[g, j] = jnp.zeros((TOK, 256), BF)
-
-            sib_grad(g, j).start()
+                tosib[g, k] = jnp.zeros((TOK, 256), BF)
+
+            sib_grad(g, k).start()
             return carry
 
-        def for_me(j, carry):
-            block = lane(z - g, j)
+        def for_me(i, carry):
+            k = 1 - i
+            block = lane(z - g, piece(k))
 
             @pl.when(block <= s)
             def _():
                 def write(gk, gv):
-                    mine[g, j, :, :HD] = gk
-                    mine[g, j, :, HD:] = gv
+                    mine[g, k, :, :HD] = gk
+                    mine[g, k, :, HD:] = gv
 
                 backward(block, write)
 
             @pl.when(block > s)
             def _():
-                mine[g, j] = jnp.zeros((TOK, 256), F32)
+                mine[g, k] = jnp.zeros((TOK, 256), F32)
+
+            @pl.when(k == 1)
+            def _():
+                sib_grad(g, 1).wait_recv()
+                for h in range(2):
+                    xout[g, h] = (mine[g, 1, halves[h]] + fromsib[g, 1, halves[h]].astype(F32)).astype(BF)
+                    x_grad(g, h).start()
 
             return carry
 
@@ -425,29 +464,33 @@
         def _():
             contributions(g)
 
+    def collect(g, h):
+        if h == 0:
+            sib_grad(g, 0).wait_recv()
+        x_grad(g, h).wait_recv()
+        half = halves[h]
+        mine[g, 0, half] += fromsib[g, 0, half].astype(F32) + xin[g, h].astype(F32)
+
+        @pl.when(up_needs(g))
+        def _():
+            ring_in(g, h).wait_recv()
+            mine[g, 0, half] += ringin[g, h].astype(F32)
+
     def send_sum(g):
         @pl.when(needed(z - g, z))
         def _():
-            for k in (1, 0):
-                j = piece(k)
-                sib_grad(g, j).wait_recv()
-                mine[g, j] += fromsib[g, j].astype(F32)
-
-                @pl.when(up_needs(g))
-                def _():
-                    ring_in(g, k).wait_recv()
-                    mine[g, j] += ringin[g, k].astype(F32)
-
-                ringout[g - 1, k] = mine[g, j].astype(BF)
-                ring_out(g, k, g in (1, 5)).start()
+            for h in range(2):
+                collect(g, h)
+                ringout[g - 1, h] = mine[g, 0, halves[h]].astype(BF)
+                ring_out(g, h, near if g == 5 else dn).start()
 
     contribute(4)
     send_sum(4)
     contribute(3)
+    contribute(2)
+    send_sum(3)
     contribute(5)
     send_sum(5)
-    send_sum(3)
-    contribute(2)
     send_sum(2)
     contribute(1)
     send_sum(1)
@@ -531,13 +574,6 @@
 
     push_q, push_q_for, step_q, cross_q, meet_q, drain_q = weight(0, anchor, (3, 4))
     push_kv, push_kv_for, step_kv, cross_kv, meet_kv, drain_kv = weight(1, projected, (4, 3))
-    for k in (1, 0):
-        sib_grad(0, piece(k)).wait_recv()
-        mine[0, piece(k)] += fromsib[0, piece(k)].astype(F32)
-        if k == 1:
-            xout[...] = mine[0, piece(1)].astype(BF)
-            x_rows = remote(xout, xin, xg_s, xg_r, xp)
-            x_rows.start()
     for h in range(2):
         grads[0, :, h * HD:(h + 1) * HD] = dq_t[:, h * TOK:(h + 1) * TOK].T.astype(BF)
     push_q_for(0)
@@ -546,25 +582,18 @@
     push_q_for(2)
     push_q_for(3)
     push_q(z)
-    x_rows.wait_recv()
-    own = mine[0, xh] + xin[...].astype(F32)
-    mine[0, xh] = own
-    for k in range(2):
+    for h in range(2):
         @pl.when(far_needs)
         def _():
-            ring_in(4, k).wait_recv()
-            mine[0, xh] += ringin[4, k].astype(F32)
-
-    for k in range(2):
-        @pl.when(up_needs(0))
-        def _():
-            ring_in(0, k).wait_recv()
-            mine[0, xh] += ringin[0, k].astype(F32)
-
-    grads[1] = mine[0, xh].astype(BF)
+            ring_in(4, h).wait_recv()
+            mine[0, 0, halves[h]] += ringin[4, h].astype(F32)
+
+        collect(0, h)
+        grads[1, halves[h]] = mine[0, 0, halves[h]].astype(BF)
+
     push_kv_for(0)
+    step_kv(0)
     push_kv_for(1)
-    step_kv(0)
     step_q(1)
     push_kv_for(2)
     step_kv(1)
@@ -585,13 +614,10 @@
         gkv_ref[pl.ds(half, 144, stride=2), :] = wacc[1, 0, :, half * HD:(half + 1) * HD]
 
     for h in range(2):
-        to_xp(h).wait_send()
-        for j in range(2):
-            @pl.when(far_needs)
-            def _():
-                to_far(j, h).wait_send()
-
-    x_rows.wait_send()
+        @pl.when(far_needs)
+        def _():
+            to_far(h).wait_send()
+
     drain_q()
     drain_kv()
     aug.drain()
@@ -604,18 +630,20 @@
     def drained(g, carry):
         @pl.when(needed(z - g, z))
         def _():
-            for j in range(2):
-                sib_grad(g, j).wait_send()
-                for h in range(2):
-                    to_sib(g, j, h).wait_send()
-
-                    @pl.when(up_needs(g))
-                    def _():
-                        to_up(g, j, h).wait_send()
+            for h in range(2):
+                sib_grad(g, h).wait_send()
+                x_grad(g, h).wait_send()
+                to_xp(g, h).wait_send()
+                for k in range(2):
+                    to_sib(g, k, h).wait_send()
+
+                @pl.when(up_needs(g))
+                def _():
+                    to_up(g, h).wait_send()
 
                 @pl.when(g > 0)
                 def _():
-                    ring_out(g, j).wait_send()
+                    ring_out(g, h).wait_send()
 
         return carry
 
@@ -651,8 +679,8 @@
             pltpu.VMEM((1, 512), F32), pltpu.VMEM((HD, 512), F32),
             pltpu.VMEM((6, 2, TOK, 256), F32),
             pltpu.VMEM((6, 2, TOK, 256), BF), pltpu.VMEM((6, 2, TOK, 256), BF),
-            pltpu.VMEM((5, 2, TOK, 256), BF), pltpu.VMEM((5, 2, TOK, 256), BF),
-            pltpu.VMEM((TOK, 256), BF), pltpu.VMEM((TOK, 256), BF),
+            pltpu.VMEM((5, 2, HALF, 256), BF), pltpu.VMEM((5, 2, HALF, 256), BF),
+            pltpu.VMEM((6, 2, HALF, 256), BF), pltpu.VMEM((6, 2, HALF, 256), BF),
             pltpu.VMEM((2, TOK, 256), BF),
             pltpu.VMEM((2, 8, 2, 144, 256), BF), pltpu.VMEM((2, 8, 2, 144, 256), BF),
             pltpu.VMEM((2, 4, 2, 144, 256), BF), pltpu.VMEM((2, 4, 2, 144, 256), BF),
@@ -660,7 +688,7 @@
             pltpu.VMEM((2, 144, 256), BF), pltpu.VMEM((2, 144, 256), BF),
             pltpu.VMEM((2, 2, 144, 256), F32),
             dma((3,)), *two((13,)), *two((13,)), *two((2, 13)), *two((5,)),
-            *two((5, 2, 2)), *two((6, 2, 2)), *two((2,)), *two((6, 2)), *two((5, 2)), *two(()),
+            *two((5, 2)), *two((6, 2, 2)), *two((6, 2)), *two((6, 2)), *two((5, 2)), *two((6, 2)),
             *two((2, 8)), *two((2, 4, 2)), *two((2, 4, 2)), *two((2,)),
         ],
         compiler_params=pltpu.CompilerParams(

time: 147 us -> 155 us (1.054)
  Pallas kernels: 145 us -> 152 us
    pallas_call x1, Pallas kernels: 143 us -> 150 us  [step_call(): pl.pallas_call(step_kernel, out_shape=[jax.ShapeDtypeStruct((TOK, 256), B...]
where the time goes in v5:
time: 155 us; the launch traced here: 153 us
  Pallas kernels  152 us (98%)
    pallas_call x1, Pallas kernels, step_call(): pl.pallas_call(step_kernel, out_shape=[jax.ShapeDtypeStruct((TOK, 256), B...  150 us

profile of v5, /device:TPU:8, one launch (start us, length us, event | category | flops | bytes accessed | tf_op | source)
XLA Modules:
  0.0 152.8 jit_solution(15052044022304816739)
XLA Ops:
  0.6 150.2 %shard_map.102 = (bf16[256,256]{1,0:T(8,128)(2,1)}, f32[144,256]{1,0:T(8,128)}, f32[288,128]{1,0:T(8,128)}, bf16[512,128]{1,0:T(8,128)(2,1)}) custom-call(bf16[288,256]{1,0:T(8,128)(2,1)} %bitcast.14, bf16[576,256]{1,0:T(8,128)(2,1)} %bitcast.13, bf16[576,2304]{1,0:T(8,128)(2,1)} %bitcast.11, bf16[4608,256]{1,0:T(8,128)(2,1)} %qw_hbm.1, ...), custom_call_target="tpu_custom_call" | custom-call | tf_op jit(solution)/shard_map/pallas_call | solution.py:658
  150.8 1.9 %shard_map.103 = (bf16[256,256]{1,0:T(8,128)(2,1)}, f32[144,256]{1,0:T(8,128)}, f32[288,128]{1,0:T(8,128)}, bf16[512,128]{1,0:T(8,128)(2,1)}) custom-call(bf16[256,256]{1,0:T(8,128)(2,1)} %get-tuple-element.12.refs_0_, f32[144,256]{1,0:T(8,128)} %get-tuple-element.13.refs_1_, f32[288,128]{1,0:T(8,128)} %get-tuple-element.14.refs_2_, ...), custom_call_target="tpu_custom_call" | custom-call | tf_op jit(solution)/shard_map/pallas_call | solution.py:711

commit v6 on v5

--- a/solution.py
+++ b/solution.py
@@ -11,6 +11,7 @@
 F32 = jnp.float32
 TOK = 256
 HALF = 128
+GROUP = 1024
 HD = 128
 MESH = pl.DeviceIdType.MESH
 LOG2E = 1.4426950408889634
@@ -115,7 +116,7 @@
     att_ref, gq_ref, gkv_ref, rows_ref,
     augment, anchor, projected, pw, qw, kw, kw_pairs, pairs, acc, kv_ref, cnt_out, cnt_in,
     kvs, q_n, q_t, do_n, do_t, num, den, first, place, delta, dq_t,
-    mine, tosib, fromsib, ringout, ringin, xout, xin, grads,
+    mine, parts, tosib, fromsib, ringout, ringin, xout, xin, grads,
     wsib_out, wsib_in, wd_out, wd_in, wu_out, wu_in, wx_out, wx_in, wacc,
     wsem, asend, arecv, nsend, nrecv, psend, precv, csend, crecv,
     up_s, up_r, sb_s, sb_r, xp_s, xp_r, gs_s, gs_r, rg_s, rg_r, xg_s, xg_r,
@@ -150,7 +151,7 @@
     ring = [up, dn, far, near]
     greet(
         [{"mp": aug.p}, {"mp": aug.up}, {"mp": aug.dn}] + ring
-        + [{"seq": one["seq"] + across} for one in ring[:2]] + [{"seq": h} for h in hyper]
+        + [{"seq": one["seq"] + across} for one in ring] + [{"seq": h} for h in hyper]
     )
 
     aug.start()
@@ -314,26 +315,19 @@
     dq_t[...] = jnp.zeros_like(dq_t)
     crossed(0, 0)
 
-    def scores(block):
-        k, v = kvs[block, :, :HD], kvs[block, :, HD:]
+    def scores(g):
+        base = 4 * (z - g)
+        kv = kvs[pl.ds(base, 4)].reshape(GROUP, 256)
+        k, v = kv[:, :HD], kv[:, HD:]
         th = jnp.tanh(dot(k, q_t[...]) * (1.0 / 600.0))
-        pos = block * TOK + lax.broadcasted_iota(jnp.int32, (TOK, 2 * TOK), 0)
-        allowed = (pos >= first[...]) & (pos <= place[...])
+        pos = lax.broadcasted_iota(jnp.int32, (GROUP, 2 * TOK), 0)
+        allowed = (pos >= first[...] - base * TOK) & (pos <= place[...] - base * TOK)
         return k, v, th, jnp.where(allowed, jnp.exp2(th * (50.0 * LOG2E)), 0.0)
 
     def forward(g):
-        def one(b, carry):
-            block = 4 * (z - g) + b
-
-            @pl.when(block <= s)
-            def _():
-                _, v, _, w = scores(block)
-                den[...] += jnp.sum(w, axis=0, keepdims=True)
-                num[...] += dot_tn(v, w.astype(BF))
-
-            return carry
-
-        lax.fori_loop(0, 4, one, 0)
+        _, v, _, w = scores(g)
+        den[...] += jnp.sum(w, axis=0, keepdims=True)
+        num[...] += dot_tn(v, w.astype(BF))
 
     acc[...] = jnp.zeros_like(acc)
     for block in (m, anc.dn, anc.up):
@@ -391,109 +385,61 @@
     def there(where, k):
         return {"seq": where["seq"] + k * across}
 
-    def ring_out(g, h, where=dn):
-        return remote(ringout.at[g - 1, h], ringin.at[g - 1, h], rg_s.at[g - 1, h], rg_r.at[g - 1, h], where)
-
-    def ring_in(g, h):
-        return remote(ringout.at[g, h], ringin.at[g, h], rg_s.at[g, h], rg_r.at[g, h], up)
+    def ring_out(g, k, h, last=False):
+        where = there(near if g == 5 else dn, k) if last else dn
+        return remote(
+            ringout.at[g - 1, k, h], ringin.at[g - 1, k, h], rg_s.at[g - 1, k, h], rg_r.at[g - 1, k, h], where
+        )
+
+    def ring_in(g, k, h):
+        return remote(ringout.at[g, k, h], ringin.at[g, k, h], rg_s.at[g, k, h], rg_r.at[g, k, h], up)
 
     def sib_grad(g, k):
         return remote(tosib.at[g, k], fromsib.at[g, k], gs_s.at[g, k], gs_r.at[g, k], sib)
 
-    def x_grad(g, h):
-        return remote(xout.at[g, h], xin.at[g, h], xg_s.at[g, h], xg_r.at[g, h], xp)
-
-    def backward(block, write):
-        k, v, th, w = scores(block)
-        prob = w * den[...]
-        soft = prob * (dot(v, do_t[...]) - delta[...])
-        raw = (soft * ((1.0 - th * th) * (1.0 / 12.0))).astype(BF)
-        write(dot(raw, q_n[...]), dot(prob.astype(BF), do_n[...]))
-        dq_t[...] += dot_tn(k, raw)
-
-    def contributions(g):
-        def for_sib(i, carry):
-            k = 1 - i
-            block = 4 * (z - g) + 2 * piece(k) + 1 - c
-
-            @pl.when(block <= s)
-            def _():
-                def write(gk, gv):
-                    tosib[g, k, :, :HD] = gk.astype(BF)
-                    tosib[g, k, :, HD:] = gv.astype(BF)
-
-                backward(block, write)
-
-            @pl.when(block > s)
-            def _():
-                tosib[g, k] = jnp.zeros((TOK, 256), BF)
-
-            sib_grad(g, k).start()
-            return carry
-
-        def for_me(i, carry):
-            k = 1 - i
-            block = lane(z - g, piece(k))
-
-            @pl.when(block <= s)
-            def _():
-                def write(gk, gv):
-                    mine[g, k, :, :HD] = gk
-                    mine[g, k, :, HD:] = gv
-
-                backward(block, write)
-
-            @pl.when(block > s)
-            def _():
-                mine[g, k] = jnp.zeros((TOK, 256), F32)
-
-            @pl.when(k == 1)
-            def _():
-                sib_grad(g, 1).wait_recv()
-                for h in range(2):
-                    xout[g, h] = (mine[g, 1, halves[h]] + fromsib[g, 1, halves[h]].astype(F32)).astype(BF)
-                    x_grad(g, h).start()
-
-            return carry
-
-        lax.fori_loop(0, 2, for_sib, 0)
-        lax.fori_loop(0, 2, for_me, 0)
-
     def contribute(g):
         @pl.when(needed(z - g, z))
         def _():
-            contributions(g)
-
-    def collect(g, h):
-        if h == 0:
-            sib_grad(g, 0).wait_recv()
-        x_grad(g, h).wait_recv()
-        half = halves[h]
-        mine[g, 0, half] += fromsib[g, 0, half].astype(F32) + xin[g, h].astype(F32)
-
-        @pl.when(up_needs(g))
-        def _():
-            ring_in(g, h).wait_recv()
-            mine[g, 0, half] += ringin[g, h].astype(F32)
+            k, v, th, w = scores(g)
+            prob = w * den[...]
+            soft = prob * (dot(v, do_t[...]) - delta[...])
+            raw = (soft * ((1.0 - th * th) * (1.0 / 12.0))).astype(BF)
+            parts[:, :HD] = dot(raw, q_n[...])
+            parts[:, HD:] = dot(prob.astype(BF), do_n[...])
+            for q in (1, 0):
+                start = (2 * piece(q) + 1 - c) * TOK
+                tosib[g, q] = parts[pl.ds(pl.multiple_of(start, TOK), TOK), :].astype(BF)
+                sib_grad(g, q).start()
+            for q in (1, 0):
+                start = (2 * piece(q) + c) * TOK
+                mine[g, q] = parts[pl.ds(pl.multiple_of(start, TOK), TOK), :]
+            dq_t[...] += dot_tn(k, raw)
 
     def send_sum(g):
         @pl.when(needed(z - g, z))
         def _():
-            for h in range(2):
-                collect(g, h)
-                ringout[g - 1, h] = mine[g, 0, halves[h]].astype(BF)
-                ring_out(g, h, near if g == 5 else dn).start()
+            for k in (1, 0):
+                sib_grad(g, k).wait_recv()
+                for h, half in enumerate(halves):
+                    mine[g, k, half] += fromsib[g, k, half].astype(F32)
+
+                    @pl.when(up_needs(g))
+                    def _():
+                        ring_in(g, k, h).wait_recv()
+                        mine[g, k, half] += ringin[g, k, h].astype(F32)
+
+                    ringout[g - 1, k, h] = mine[g, k, half].astype(BF)
+                    ring_out(g, k, h, g in (1, 5)).start()
 
     contribute(4)
     send_sum(4)
     contribute(3)
     contribute(2)
     send_sum(3)
+    contribute(1)
     contribute(5)
     send_sum(5)
     send_sum(2)
-    contribute(1)
-    send_sum(1)
     contribute(0)
 
     def weight(n, act, lengths):
@@ -572,39 +518,52 @@
 
         return push, push_for, step, cross, meet, drain
 
-    push_q, push_q_for, step_q, cross_q, meet_q, drain_q = weight(0, anchor, (3, 4))
+    push_q, push_q_for, step_q, cross_q, meet_q, drain_q = weight(0, anchor, (2, 5))
     push_kv, push_kv_for, step_kv, cross_kv, meet_kv, drain_kv = weight(1, projected, (4, 3))
+    x_rows = remote(xout, xin, xg_s, xg_r, xp)
+    sib_grad(0, 1).wait_recv()
+    xout[...] = (mine[0, 1] + fromsib[0, 1].astype(F32)).astype(BF)
+    x_rows.start()
     for h in range(2):
         grads[0, :, h * HD:(h + 1) * HD] = dq_t[:, h * TOK:(h + 1) * TOK].T.astype(BF)
     push_q_for(0)
     push_q_for(1)
+    send_sum(1)
     step_q(0)
-    push_q_for(2)
-    push_q_for(3)
+    for k in range(2, 5):
+        push_q_for(k)
     push_q(z)
-    for h in range(2):
-        @pl.when(far_needs)
-        def _():
-            ring_in(4, h).wait_recv()
-            mine[0, 0, halves[h]] += ringin[4, h].astype(F32)
-
-        collect(0, h)
-        grads[1, halves[h]] = mine[0, 0, halves[h]].astype(BF)
-
+    step_q(1)
+    sib_grad(0, 0).wait_recv()
+    x_rows.wait_recv()
+    mine[0, 0] += fromsib[0, 0].astype(F32) + xin[...].astype(F32)
+    for k in (1, 0):
+        for h, half in enumerate(halves):
+            @pl.when(far_needs)
+            def _():
+                ring_in(4, k, h).wait_recv()
+                mine[0, 0, half] += ringin[4, k, h].astype(F32)
+
+            @pl.when(up_needs(0))
+            def _():
+                ring_in(0, k, h).wait_recv()
+                mine[0, 0, half] += ringin[0, k, h].astype(F32)
+
+    grads[1] = mine[0, 0].astype(BF)
     push_kv_for(0)
     step_kv(0)
     push_kv_for(1)
-    step_q(1)
     push_kv_for(2)
+    step_q(2)
     step_kv(1)
-    step_q(2)
     push_kv_for(3)
     push_kv(z)
+    step_q(3)
     step_kv(2)
     cross_kv()
     cross_q()
     step_kv(3)
-    step_q(3)
+    step_q(4)
     for half in range(2):
         pairs[pl.ds(half, TOK, stride=2), :] = grads[1, :, half * HD:(half + 1) * HD].astype(F32)
     rows_ref[...] = pairs[:2 * TOK, :].astype(BF)
@@ -618,6 +577,7 @@
         def _():
             to_far(h).wait_send()
 
+    x_rows.wait_send()
     drain_q()
     drain_kv()
     aug.drain()
@@ -632,7 +592,6 @@
         def _():
             for h in range(2):
                 sib_grad(g, h).wait_send()
-                x_grad(g, h).wait_send()
                 to_xp(g, h).wait_send()
                 for k in range(2):
                     to_sib(g, k, h).wait_send()
@@ -643,7 +602,8 @@
 
                 @pl.when(g > 0)
                 def _():
-                    ring_out(g, h).wait_send()
+                    for k in range(2):
+                        ring_out(g, k, h).wait_send()
 
         return carry
 
@@ -677,19 +637,19 @@
             pltpu.VMEM((HD, 512), F32), pltpu.VMEM((1, 512), F32),
             pltpu.VMEM((1, 512), jnp.int32), pltpu.VMEM((1, 512), jnp.int32),
             pltpu.VMEM((1, 512), F32), pltpu.VMEM((HD, 512), F32),
-            pltpu.VMEM((6, 2, TOK, 256), F32),
+            pltpu.VMEM((6, 2, TOK, 256), F32), pltpu.VMEM((GROUP, 256), F32),
             pltpu.VMEM((6, 2, TOK, 256), BF), pltpu.VMEM((6, 2, TOK, 256), BF),
-            pltpu.VMEM((5, 2, HALF, 256), BF), pltpu.VMEM((5, 2, HALF, 256), BF),
-            pltpu.VMEM((6, 2, HALF, 256), BF), pltpu.VMEM((6, 2, HALF, 256), BF),
+            pltpu.VMEM((5, 2, 2, HALF, 256), BF), pltpu.VMEM((5, 2, 2, HALF, 256), BF),
+            pltpu.VMEM((TOK, 256), BF), pltpu.VMEM((TOK, 256), BF),
             pltpu.VMEM((2, TOK, 256), BF),
             pltpu.VMEM((2, 8, 2, 144, 256), BF), pltpu.VMEM((2, 8, 2, 144, 256), BF),
             pltpu.VMEM((2, 4, 2, 144, 256), BF), pltpu.VMEM((2, 4, 2, 144, 256), BF),
-            pltpu.VMEM((2, 4, 2, 144, 256), BF), pltpu.VMEM((2, 4, 2, 144, 256), BF),
+            pltpu.VMEM((2, 5, 2, 144, 256), BF), pltpu.VMEM((2, 5, 2, 144, 256), BF),
             pltpu.VMEM((2, 144, 256), BF), pltpu.VMEM((2, 144, 256), BF),
             pltpu.VMEM((2, 2, 144, 256), F32),
             dma((3,)), *two((13,)), *two((13,)), *two((2, 13)), *two((5,)),
-            *two((5, 2)), *two((6, 2, 2)), *two((6, 2)), *two((6, 2)), *two((5, 2)), *two((6, 2)),
-            *two((2, 8)), *two((2, 4, 2)), *two((2, 4, 2)), *two((2,)),
+            *two((5, 2)), *two((6, 2, 2)), *two((6, 2)), *two((6, 2)), *two((5, 2, 2)), *two(()),
+            *two((2, 8)), *two((2, 4, 2)), *two((2, 5, 2)), *two((2,)),
         ],
         compiler_params=pltpu.CompilerParams(
             collective_id=1, has_side_effects=True, vmem_limit_bytes=60 * 1024 * 1024

time: 155 us -> 145 us (0.935); the launches traced: 153 us -> 145 us
  Pallas kernels: 152 us -> 144 us
    pallas_call x1, Pallas kernels: 150 us -> 142 us  [step_call(): pl.pallas_call(step_kernel, out_shape=[jax.ShapeDtypeStruct((TOK, 256), B...]
where the time goes in v6:
time: 145 us
  Pallas kernels  144 us (99%)
    pallas_call x1, Pallas kernels, step_call(): pl.pallas_call(step_kernel, out_shape=[jax.ShapeDtypeStruct((TOK, 256), B...  142 us

profile of v6, /device:TPU:8, one launch (start us, length us, event | category | flops | bytes accessed | tf_op | source)
XLA Modules:
  0.0 144.9 jit_solution(17532503476614589885)
XLA Ops:
  0.6 142.4 %shard_map.102 = (bf16[256,256]{1,0:T(8,128)(2,1)}, f32[144,256]{1,0:T(8,128)}, f32[288,128]{1,0:T(8,128)}, bf16[512,128]{1,0:T(8,128)(2,1)}) custom-call(bf16[288,256]{1,0:T(8,128)(2,1)} %bitcast.14, bf16[576,256]{1,0:T(8,128)(2,1)} %bitcast.13, bf16[576,2304]{1,0:T(8,128)(2,1)} %bitcast.11, bf16[4608,256]{1,0:T(8,128)(2,1)} %qw_hbm.1, ...), custom_call_target="tpu_custom_call" | custom-call | tf_op jit(solution)/shard_map/pallas_call | solution.py:618
  143.0 1.9 %shard_map.103 = (bf16[256,256]{1,0:T(8,128)(2,1)}, f32[144,256]{1,0:T(8,128)}, f32[288,128]{1,0:T(8,128)}, bf16[512,128]{1,0:T(8,128)(2,1)}) custom-call(bf16[256,256]{1,0:T(8,128)(2,1)} %get-tuple-element.12.refs_0_, f32[144,256]{1,0:T(8,128)} %get-tuple-element.13.refs_1_, f32[288,128]{1,0:T(8,128)} %get-tuple-element.14.refs_2_, ...), custom_call_target="tpu_custom_call" | custom-call | tf_op jit(solution)/shard_map/pallas_call | solution.py:671

commit v7 on v6

--- a/solution.py
+++ b/solution.py
@@ -198,6 +198,8 @@
     own_projected[...] = dot(pw[...], augment[...]).astype(BF)
     pros[0].start()
     count(0)
+    for stage in range(3):
+        anc.relay(stage)
     lax.fori_loop(6, 8, unpair, 0)
 
     def add(block):
@@ -288,8 +290,6 @@
     add_kv(0, m)
     gather(0, 0, 1, 2, 3, 4)
     pros[1].start()
-    for stage in range(3):
-        anc.relay(stage)
     count(1)
     add_kv(1, m)
     gather(0, 5, 6, 7)
@@ -297,10 +297,10 @@
     gather(0, 8)
     launch(0)
     count(2)
+    for stage in range(3, 6):
+        anc.relay(stage)
     gather(1, 1, 2, 3, 4)
     pass_on(1, 0)
-    for stage in range(3, 6):
-        anc.relay(stage)
     count(3)
     gather(1, 5, 6)
     pass_on(2, 0)
@@ -518,7 +518,7 @@
 
         return push, push_for, step, cross, meet, drain
 
-    push_q, push_q_for, step_q, cross_q, meet_q, drain_q = weight(0, anchor, (2, 5))
+    push_q, push_q_for, step_q, cross_q, meet_q, drain_q = weight(0, anchor, (3, 4))
     push_kv, push_kv_for, step_kv, cross_kv, meet_kv, drain_kv = weight(1, projected, (4, 3))
     x_rows = remote(xout, xin, xg_s, xg_r, xp)
     sib_grad(0, 1).wait_recv()
@@ -530,10 +530,11 @@
     push_q_for(1)
     send_sum(1)
     step_q(0)
-    for k in range(2, 5):
-        push_q_for(k)
+    push_q_for(2)
+    push_q_for(3)
     push_q(z)
     step_q(1)
+    step_q(2)
     sib_grad(0, 0).wait_recv()
     x_rows.wait_recv()
     mine[0, 0] += fromsib[0, 0].astype(F32) + xin[...].astype(F32)
@@ -554,7 +555,6 @@
     step_kv(0)
     push_kv_for(1)
     push_kv_for(2)
-    step_q(2)
     step_kv(1)
     push_kv_for(3)
     push_kv(z)
@@ -563,7 +563,6 @@
     cross_kv()
     cross_q()
     step_kv(3)
-    step_q(4)
     for half in range(2):
         pairs[pl.ds(half, TOK, stride=2), :] = grads[1, :, half * HD:(half + 1) * HD].astype(F32)
     rows_ref[...] = pairs[:2 * TOK, :].astype(BF)

time: 145 us -> 149 us (1.028)
  Pallas kernels: 144 us -> 147 us
    pallas_call x1, Pallas kernels: 142 us -> 145 us  [step_call(): pl.pallas_call(step_kernel, out_shape=[jax.ShapeDtypeStruct((TOK, 256), B...]
where the time goes in v7:
time: 149 us; the launch traced here: 148 us
  Pallas kernels  147 us (99%)
    pallas_call x1, Pallas kernels, step_call(): pl.pallas_call(step_kernel, out_shape=[jax.ShapeDtypeStruct((TOK, 256), B...  145 us

profile of v7, /device:TPU:8, one launch (start us, length us, event | category | flops | bytes accessed | tf_op | source)
XLA Modules:
  0.0 147.7 jit_solution(2178122871000297574)
XLA Ops:
  0.6 145.1 %shard_map.102 = (bf16[256,256]{1,0:T(8,128)(2,1)}, f32[144,256]{1,0:T(8,128)}, f32[288,128]{1,0:T(8,128)}, bf16[512,128]{1,0:T(8,128)(2,1)}) custom-call(bf16[288,256]{1,0:T(8,128)(2,1)} %bitcast.14, bf16[576,256]{1,0:T(8,128)(2,1)} %bitcast.13, bf16[576,2304]{1,0:T(8,128)(2,1)} %bitcast.11, bf16[4608,256]{1,0:T(8,128)(2,1)} %qw_hbm.1, ...), custom_call_target="tpu_custom_call" | custom-call | tf_op jit(solution)/shard_map/pallas_call | solution.py:617
  145.8 1.9 %shard_map.103 = (bf16[256,256]{1,0:T(8,128)(2,1)}, f32[144,256]{1,0:T(8,128)}, f32[288,128]{1,0:T(8,128)}, bf16[512,128]{1,0:T(8,128)(2,1)}) custom-call(bf16[256,256]{1,0:T(8,128)(2,1)} %get-tuple-element.12.refs_0_, f32[144,256]{1,0:T(8,128)} %get-tuple-element.13.refs_1_, f32[288,128]{1,0:T(8,128)} %get-tuple-element.14.refs_2_, ...), custom_call_target="tpu_custom_call" | custom-call | tf_op jit(solution)/shard_map/pallas_call | solution.py:670

commit v8 on v6

--- a/solution.py
+++ b/solution.py
@@ -518,7 +518,7 @@
 
         return push, push_for, step, cross, meet, drain
 
-    push_q, push_q_for, step_q, cross_q, meet_q, drain_q = weight(0, anchor, (2, 5))
+    push_q, push_q_for, step_q, cross_q, meet_q, drain_q = weight(0, anchor, (3, 4))
     push_kv, push_kv_for, step_kv, cross_kv, meet_kv, drain_kv = weight(1, projected, (4, 3))
     x_rows = remote(xout, xin, xg_s, xg_r, xp)
     sib_grad(0, 1).wait_recv()
@@ -530,8 +530,8 @@
     push_q_for(1)
     send_sum(1)
     step_q(0)
-    for k in range(2, 5):
-        push_q_for(k)
+    push_q_for(2)
+    push_q_for(3)
     push_q(z)
     step_q(1)
     sib_grad(0, 0).wait_recv()
@@ -563,7 +563,6 @@
     cross_kv()
     cross_q()
     step_kv(3)
-    step_q(4)
     for half in range(2):
         pairs[pl.ds(half, TOK, stride=2), :] = grads[1, :, half * HD:(half + 1) * HD].astype(F32)
     rows_ref[...] = pairs[:2 * TOK, :].astype(BF)

time: 145 us -> 144 us (level)
  no operation moved by 1% of the time
where the time goes in v8:
time: 144 us
  Pallas kernels  144 us (100%)
    pallas_call x1, Pallas kernels, step_call(): pl.pallas_call(step_kernel, out_shape=[jax.ShapeDtypeStruct((TOK, 256), B...  142 us

profile of v8, /device:TPU:8, one launch (start us, length us, event | category | flops | bytes accessed | tf_op | source)
XLA Modules:
  0.0 144.3 jit_solution(1297778840855371327)
XLA Ops:
  0.6 141.7 %shard_map.102 = (bf16[256,256]{1,0:T(8,128)(2,1)}, f32[144,256]{1,0:T(8,128)}, f32[288,128]{1,0:T(8,128)}, bf16[512,128]{1,0:T(8,128)(2,1)}) custom-call(bf16[288,256]{1,0:T(8,128)(2,1)} %bitcast.14, bf16[576,256]{1,0:T(8,128)(2,1)} %bitcast.13, bf16[576,2304]{1,0:T(8,128)(2,1)} %bitcast.11, bf16[4608,256]{1,0:T(8,128)(2,1)} %qw_hbm.1, ...), custom_call_target="tpu_custom_call" | custom-call | tf_op jit(solution)/shard_map/pallas_call | solution.py:617
  142.3 1.9 %shard_map.103 = (bf16[256,256]{1,0:T(8,128)(2,1)}, f32[144,256]{1,0:T(8,128)}, f32[288,128]{1,0:T(8,128)}, bf16[512,128]{1,0:T(8,128)(2,1)}) custom-call(bf16[256,256]{1,0:T(8,128)(2,1)} %get-tuple-element.12.refs_0_, f32[144,256]{1,0:T(8,128)} %get-tuple-element.13.refs_1_, f32[288,128]{1,0:T(8,128)} %get-tuple-element.14.refs_2_, ...), custom_call_target="tpu_custom_call" | custom-call | tf_op jit(solution)/shard_map/pallas_call | solution.py:670
